TPU v7x, 32 devices: a whole 2x2x4 slice. The times are simulated.
32 devices in a mesh: sub: 8 (over z, x), blk: 4 (over y, core).
Axes of the slice: x: 2, y: 2, z: 4, core: 2. Of those that a mesh axis runs over, the one named last changes fastest.
Arguments:
- residual: float32 [8, 8, 375, 256], P('sub', 'blk'), may hold values from -6 to 6
- stiffness: bfloat16 [8, 8, 16, 375, 375], P('sub', 'blk'), may hold values from -0.078125 to 0.078125
- pattern: int32 [8, 8, 16], P('sub', 'blk'), may hold values from 0 to 7
- neumann_inv: bfloat16 [8, 8, 375, 375], P('sub', 'blk'), may hold values from -0.3125 to 0.3125
- dirichlet_inv: bfloat16 [8, 8, 375, 375], P('sub', 'blk'), may hold values from -0.3125 to 0.3125
- basis: bfloat16 [8, 8, 375, 192], P('sub', 'blk'), may hold values from -0.5 to 0.5
- node_ops: float32 [8, 3, 192, 192], P('sub'), as said below
- root_inv: float32 [192, 192], replicated, may hold values from -0.4375 to 0.4375
Outputs:
- preconditioned: float32 [8, 8, 375, 256], P('sub', 'blk')
Inputs may be any that keep to these rules, and one draw needn't show every extreme that they name: node_ops[s, l] equals node_ops[t, l] whenever s // 2**l == t // 2**l: one map for each tree node, held by all of its subdomains.
All inputs are finite; a program needn't handle non-finite values.
Results may differ from a plain program's by a relative error of at most 0.004.
Values may be sent and summed in bfloat16 or wider, within the bound.
No kernel may reach another device: no remote copies, remote signals or barrier semaphores. Data moves between devices by JAX's collectives and lax.ppermute only.
A program may use at most 64 MiB of HBM per device.

v0:
```python
import functools

import jax
import jax.numpy as jnp
from jax import lax
from jax.experimental import pallas as pl
from jax.experimental.pallas import tpu as pltpu
from jax.sharding import PartitionSpec as P

BF = jnp.bfloat16
F32 = jnp.float32
VMEM = pl.BlockSpec(memory_space=pltpu.VMEM)
SMEM = pl.BlockSpec(memory_space=pltpu.SMEM)
HBM = pl.BlockSpec(memory_space=pltpu.HBM)


def route(x, subs, blks, target):
    pairs = []
    for s in range(subs):
        for b in range(blks):
            to = target(s, b)
            if to is not None and 0 <= to[0] < subs:
                pairs.append((s * blks + b, to[0] * blks + to[1]))
    return lax.ppermute(x, ("sub", "blk"), pairs)


def product(a, b, dims):
    a_high, b_high = a.astype(BF), b.astype(BF)
    a_low, b_low = (a - a_high.astype(F32)).astype(BF), (b - b_high.astype(F32)).astype(BF)
    part = functools.partial(
        lax.dot_general, dimension_numbers=(dims, ((), ())), preferred_element_type=F32
    )
    return part(a_high, b_high) + (part(a_high, b_low) + part(a_low, b_high))


def dot(a, b):
    return product(a, b, ((1,), (0,)))


def tdot(a, b):
    return product(a, b, ((0,), (0,)))


def bdot(a, b):
    return jnp.dot(a, b, preferred_element_type=F32)


def call(kernel, outs, specs, flops, moved, scratch=(), limit=16, outs_at=None):
    return pl.pallas_call(
        kernel,
        out_shape=outs,
        in_specs=specs,
        out_specs=jax.tree.map(lambda _: VMEM, outs) if outs_at is None else outs_at,
        scratch_shapes=scratch,
        compiler_params=pltpu.CompilerParams(vmem_limit_bytes=limit * 2**20),
        cost_estimate=pl.CostEstimate(flops=flops, bytes_accessed=moved, transcendentals=0),
    )


def rows_of(ref, j, part):
    rows, parts, blocks, lanes = ref.shape
    flat = ref.reshape(rows * parts * blocks, lanes)
    return flat, pl.ds(part * blocks + j, rows, stride=parts * blocks)


def start_kernel(flags_ref, residual_hbm, *refs):
    given = (len(refs) - 5) // 2
    sources, loaded = refs[:given], refs[given : 2 * given]
    scaled_ref, keep_ref, send_ref, residual_ref, sems = refs[2 * given :]
    modes_ref, maps_ref = loaded[:2]
    copies = [
        pltpu.make_async_copy(source, target, sems.at[i])
        for i, (source, target) in enumerate(zip((residual_hbm,) + sources, (residual_ref,) + loaded))
    ]
    for copy in copies:
        copy.start()
    is_even, is_edge, is_upper = (flags_ref[i] > 0 for i in range(3))
    per, _, loads = scaled_ref.shape
    lanes = residual_ref.shape[-1]
    total = jnp.zeros((modes_ref.shape[1], loads), F32)
    copies[0].wait()
    copies[1].wait()
    for j in range(per):
        is_far = is_even if j == 0 else jnp.logical_not(is_even)
        scale = jnp.where(is_edge & is_far, 1.0, 0.5).astype(F32)
        for part in range(loads // lanes):
            flat, rows = rows_of(residual_ref, j, part)
            scaled_ref[j, :, part * lanes : (part + 1) * lanes] = (flat[rows, :] * scale).astype(BF)
        total += bdot(modes_ref[j], scaled_ref[j])
    copies[2].wait()
    mapped = tdot(maps_ref[0], total)
    for i, values in enumerate((total, mapped)):
        low, high = values[:, : loads // 2], values[:, loads // 2 :]
        keep_ref[i] = jnp.where(is_upper, high, low)
        send_ref[i] = jnp.where(is_upper, low, high)
    for copy in copies[3:]:
        copy.wait()


def local_kernel(flags_ref, scaled_ref, inverse_hbm, modes_ref, near_ref, far_ref, near_out, far_out, inverse_ref, rows_ref, sem):
    copy = pltpu.make_async_copy(inverse_hbm, inverse_ref, sem)
    copy.start()
    loads = scaled_ref.shape[-1]
    is_even = flags_ref[0] > 0
    low_modes, high_modes = (modes_ref[j].T for j in range(2))
    near_out[:, loads:] = jnp.where(is_even, high_modes, low_modes)
    far_out[:, loads:] = jnp.where(is_even, low_modes, high_modes)
    copy.wait()
    rows, per, columns = inverse_ref.shape
    inverse = inverse_ref[...].reshape(rows * per, columns)
    lanes = rows_ref.shape[-1]
    products = [bdot(inverse, scaled_ref[j]) for j in range(per)]
    for part in range(loads // lanes):
        here = slice(part * lanes, (part + 1) * lanes)
        for j in range(per):
            rows_ref[j, part] = products[j][:, here]
        low, high = (rows_ref[j, part, pl.ds(j, rows, stride=per), :] for j in range(per))
        near, far = jnp.where(is_even, high, low), jnp.where(is_even, low, high)
        near_ref[:, here] = near
        far_ref[:, here] = far
        near_out[:, here] = near.astype(BF)
        far_out[:, here] = far.astype(BF)


def pair_kernel(keep_ref, got_ref, same_ref, cross_ref, map_ref, coarse_ref, pair_ref, own_ref, sent_ref, share_ref):
    coarse = keep_ref[0] + got_ref[0]
    for i in range(same_ref.shape[0]):
        coarse += same_ref[i].astype(F32)
    pair = tdot(map_ref[0], coarse)
    for i in range(cross_ref.shape[0]):
        pair += cross_ref[i].astype(F32)
    own = tdot(map_ref[1], pair)
    coarse_ref[...] = coarse
    pair_ref[...] = pair
    own_ref[...] = own
    sent_ref[...] = own.astype(BF)
    share_ref[...] = coarse.astype(BF)


def offer_kernel(coarse_ref, near_ref, near_fix_ref, map_ref, out_ref):
    loads = near_fix_ref.shape[-1]
    modes = near_ref[:, loads:]
    out_ref[:, :loads] = (near_fix_ref[...] + bdot(modes, coarse_ref[...])).astype(BF)
    high = map_ref[0].astype(BF)
    low = (map_ref[0] - high.astype(F32)).astype(BF)
    out_ref[:, loads:] = (bdot(modes, high) + bdot(modes, low)).astype(BF)


def level_kernel(level, own_ref, got_ref, map_ref, value_ref, next_ref, sent_ref):
    value = own_ref[...] + got_ref[...].astype(F32)
    value_ref[...] = value
    following = tdot(map_ref[level], value)
    next_ref[...] = following
    sent_ref[...] = following.astype(BF)


def down_kernel(own_ref, got_ref, map_ref, root_ref, coarse_ref, *refs):
    values, fields_ref = refs[:-1], refs[-1]
    field = dot(root_ref[...], own_ref[...] + got_ref[...].astype(F32))
    for level in reversed(range(1, map_ref.shape[0])):
        field = dot(map_ref[level], field) + values[level - 1][...]
    fields_ref[0] = (dot(map_ref[0], field) + coarse_ref[...]).astype(BF)
    fields_ref[1] = field.astype(BF)


def near_kernel(fields_ref, near_ref, near_in_ref, near_fix_ref, near_out, near_bf):
    loads = near_fix_ref.shape[-1]
    own = near_fix_ref[...] + bdot(near_ref[:, loads:], fields_ref[0])
    other = near_in_ref[:, :loads].astype(F32) + bdot(near_in_ref[:, loads:], fields_ref[1])
    near = 0.5 * own + 0.5 * other
    near_out[...] = near
    near_bf[...] = near.astype(BF)


def far_kernel(flags_ref, fields_ref, near_ref, far_ref, far_in_ref, far_fix_ref, far_out, far_bf, mine_bf):
    loads = far_fix_ref.shape[-1]
    field = fields_ref[0]
    scale = jnp.where(flags_ref[1] > 0, 1.0, 0.5).astype(F32)
    far = (far_fix_ref[...] + bdot(far_ref[:, loads:], field)) * scale
    far_out[...] = far
    far_bf[...] = far.astype(BF)
    mine_bf[0] = far.astype(BF)
    mine_bf[1] = near_ref[...]
    for i in range(far_in_ref.shape[0]):
        block = far_in_ref[i, :, :loads].astype(F32) + bdot(far_in_ref[i, :, loads:], field)
        mine_bf[2 + i] = (block * scale).astype(BF)


def note_slots(slots_ref, first, end, number, list_ref):
    for i in range(list_ref.shape[1]):
        list_ref[0, i], list_ref[1, i] = 0, end - first

    def note(k, found):
        slot = slots_ref[k] - first
        is_here = (slot >= 0) & (slot < end - first)

        @pl.when(is_here)
        def _():
            list_ref[0, found], list_ref[1, found] = k, slot

        return found + is_here.astype(jnp.int32)

    list_ref[2, 0] = lax.fori_loop(0, number, note, 0)


def add_products(list_ref, matrix_ref, sources, values_ref, total):
    end = 0
    for source in sources:
        values_ref[end : end + source.shape[0]] = source[...]
        end += source.shape[0]
    values_ref[end] = jnp.zeros(values_ref.shape[1:], BF)
    found = list_ref[2, 0]
    most = 8

    def add(first, width):
        places = [first + i for i in range(width)]
        matrices = jnp.concatenate([matrix_ref[list_ref[0, at]] for at in places], axis=1)
        values = jnp.concatenate([values_ref[list_ref[1, at]] for at in places], axis=0)
        total[...] += bdot(matrices, values)

    def whole(step, carry):
        add(step * most, most)
        return carry

    steps = found // most
    lax.fori_loop(0, steps, whole, 0)
    left = found - steps * most
    for width in range(2, most + 1, 2):

        @pl.when((left > width - 2) & (left <= width))
        def _():
            add(steps * most, width)


def pick_kernel(flags_ref, inverse_ref, picked_ref):
    inverse = inverse_ref[...]
    picked_ref[...] = jnp.where(flags_ref[0] > 0, inverse[:, 0, :], inverse[:, 1, :])


def couple_kernel(late, slots_ref, flags_ref, matrix_ref, mine_ref, core_ref, total_ref, late_list_ref, values_ref, list_ref):
    @pl.when(flags_ref[1] > 0)
    def _():
        total_ref[...] = jnp.zeros(total_ref.shape, F32)
        sources = mine_ref, core_ref
        here = sum(source.shape[0] for source in sources)
        number = matrix_ref.shape[0]
        note_slots(slots_ref, 0, here, number, list_ref)
        note_slots(slots_ref, here, here + late, number, late_list_ref)
        add_products(list_ref, matrix_ref, sources, values_ref, total_ref)


def finish_kernel(list_ref, flags_ref, matrix_ref, picked_ref, total_ref, late_ref, late_core_ref, far_ref, far_in_ref, near_ref, out_ref, sum_ref, values_ref):
    is_even = flags_ref[0] > 0
    is_edge = flags_ref[1] > 0

    @pl.when(is_edge)
    def _():
        sum_ref[...] = total_ref[...]
        add_products(list_ref, matrix_ref, (late_ref, late_core_ref), values_ref, sum_ref)
        sum_ref[...] = far_ref[...] - bdot(picked_ref[...], sum_ref[...].astype(BF))

    @pl.when(jnp.logical_not(is_edge))
    def _():
        sum_ref[...] = far_ref[...] + far_in_ref[...].astype(F32)

    _, parts, _, lanes = out_ref.shape
    for part in range(parts):
        columns = slice(part * lanes, (part + 1) * lanes)
        far, near = sum_ref[:, columns], near_ref[:, columns]
        for j, values in enumerate((jnp.where(is_even, far, near), jnp.where(is_even, near, far))):
            flat, rows = rows_of(out_ref, j, part)
            flat[rows, :] = values


def after(x, *others):
    return lax.optimization_barrier((x,) + others)[0]


def shards(subs, blks, residual, stiffness, pattern, neumann_inv, dirichlet_inv, basis, node_ops, root_inv):
    here = lax.axis_index("sub")
    mine = lax.axis_index("blk")
    _, per, block, loads = residual.shape
    width = basis.shape[-1]
    coupled = pattern.shape[-1]
    levels = node_ops.shape[1]
    lanes = 128
    parts = loads // lanes
    assert per == 2 and levels > 2
    even = here % 2 == 0
    edge = (here == 0) | (here == subs - 1)
    upper = mine % 2 == 1
    flags = jnp.stack([even, edge, upper]).astype(jnp.int32)
    go = functools.partial(route, subs=subs, blks=blks)
    others = range(2, blks, 2)
    shape = jax.ShapeDtypeStruct
    half_shape = width, loads // 2
    small = 2 * width * width * loads // 2
    large = 10**11

    def swap(x, sub=0, blk=0):
        return go(x, target=lambda s, b: (s ^ sub, b ^ blk))

    def joined(x):
        other = swap(x, blk=1)
        return jnp.concatenate([jnp.where(upper, other, x), jnp.where(upper, x, other)], axis=-1)

    def turned(x):
        return jnp.transpose(x[0], (1, 0, 2))

    modes = jnp.transpose(basis[0], (0, 2, 1))
    laid = jnp.transpose(residual[0].reshape(per, block, parts, lanes), (1, 2, 0, 3))

    given = modes, node_ops[0]
    modes, maps, scaled, keep, sent = call(
        start_kernel,
        tuple(shape(x.shape, x.dtype) for x in given)
        + (shape((per, block, loads), BF),)
        + (shape((2,) + half_shape, F32),) * 2,
        [SMEM] + [HBM] * (1 + len(given)),
        2 * per * block * width * loads,
        0,
        [pltpu.VMEM(laid.shape, F32), pltpu.SemaphoreType.DMA((1 + len(given),))],
        52,
    )(flags, laid, *given)
    got = swap(sent, blk=1)
    neumann = turned(neumann_inv)
    near_fix, far_fix, to_sibling, to_far = call(
        local_kernel,
        (shape((block, loads), F32),) * 2 + (shape((block, loads + width), BF),) * 2,
        [SMEM, VMEM, HBM, VMEM],
        large,
        0,
        [
            pltpu.VMEM(neumann.shape, BF),
            pltpu.VMEM((per, parts, per * block, lanes), F32),
            pltpu.SemaphoreType.DMA(()),
        ],
        16,
    )(flags, after(scaled, got), neumann, modes)
    half_bf, mapped_bf = (keep[0] + got[0]).astype(BF), (keep[1] + got[1]).astype(BF)

    same = jnp.stack([swap(half_bf, blk=d) for d in others])
    cross = jnp.stack([swap(mapped_bf, sub=1, blk=d) for d in (0,) + tuple(others)])
    cross, to_sibling, to_far = lax.optimization_barrier((cross, to_sibling, to_far))
    coarse, value, own, own_bf, share = call(
        pair_kernel,
        (shape(half_shape, F32),) * 3
        + (shape(half_shape, BF),) * 2,
        [VMEM] * 5,
        3 * small,
        8 * width * width,
        limit=4,
    )(keep, got, same, cross, maps)
    offer = call(
        offer_kernel,
        shape(to_sibling.shape, BF),
        [VMEM] * 4,
        3 * 10**9,
        0,
    )(joined(share), to_sibling, near_fix, maps)
    from_sibling = swap(offer, sub=1)
    from_others = jnp.stack([swap(to_far, blk=d) for d in others])
    values = [value]
    for level in range(2, levels):
        value, own, own_bf = call(
            functools.partial(level_kernel, level),
            (shape(half_shape, F32),) * 2 + (shape(half_shape, BF),),
            [VMEM] * 3,
            2*10**9,
            4 * width * width,
            limit=4,
        )(own, swap(own_bf, sub=2 ** (level - 1)), maps)
        values.append(value)
    fields = call(
        down_kernel,
        shape((2,) + half_shape, BF),
        [VMEM] * (5 + len(values)),
        (levels + 3) * small,
        4 * (levels + 2) * width * width,
        limit=4,
    )(own, swap(own_bf, sub=subs // 2), maps, root_inv, coarse, *values)
    far_id = jnp.where(even, 0, per - 1)
    matrix = lax.dynamic_index_in_dim(stiffness[0], after(far_id, own_bf), 0, False)
    fields, from_sibling, from_others, matrix = lax.optimization_barrier(
        (fields, from_sibling, from_others, matrix)
    )
    fields = joined(fields)

    count = 2 + len(others)
    face = 2 * block * width * loads
    near, near_bf = call(
        near_kernel,
        (shape((block, loads), F32), shape((block, loads), BF)),
        [VMEM] * 4,
        2 * face,
        block * loads * 8,
    )(fields, to_sibling, from_sibling, near_fix)
    late = jnp.stack(
        [
            go(near_bf, target=lambda s, b, d=d: (s, b ^ d) if s in (0, subs - 1) else (s, b ^ 1))
            for d in others
        ]
    )
    far, far_bf, mine_bf = call(
        far_kernel,
        (shape((block, loads), F32), shape((block, loads), BF), shape((count, block, loads), BF)),
        [SMEM] + [VMEM] * 5,
        10**11,
        count * block * loads * 8,
    )(flags, fields, near_bf, to_far, from_others, far_fix)

    core = swap(mine_bf, blk=1)
    picked = call(
        pick_kernel,
        shape((block, block), BF),
        [SMEM, VMEM],
        1000,
        0,
    )(after(flags, near_bf), turned(dirichlet_inv))
    far_in = go(
        far_bf,
        target=lambda s, b: (s, b ^ 1) if s in (0, subs - 1) else (s - 1 if s % 2 == 0 else s + 1, b),
    )
    columns = pattern[0, far_id]
    offset = (columns // per) ^ mine
    is_near = columns % per != far_id
    distant = offset // 2
    slots = jnp.where(
        is_near & (distant > 0),
        2 * count + (offset % 2) * len(others) + distant - 1,
        (offset % 2) * count + jnp.where(is_near, 1, jnp.where(distant > 0, 1 + distant, 0)),
    )
    first = 2 * count
    more = 2 * len(others)
    listed = (3, -(-coupled // 8) * 8)
    total, late_list = call(
        functools.partial(couple_kernel, more),
        (shape((block, loads), F32), shape(listed, jnp.int32)),
        [SMEM, SMEM] + [VMEM] * 3,
        1000,
        2 * coupled * block * block,
        [pltpu.VMEM((first + 1, block, loads), BF), pltpu.SMEM(listed, jnp.int32)],
        outs_at=(VMEM, SMEM),
    )(slots, flags, matrix, mine_bf, core)
    late, total, picked = lax.optimization_barrier((late, total, picked))
    late_core = swap(late, blk=1)
    result = call(
        finish_kernel,
        shape((block, parts, per, lanes), F32),
        [SMEM, SMEM] + [VMEM] * 8,
        2 * block * block * loads,
        block * loads * 16,
        [
            pltpu.VMEM((block, loads), F32),
            pltpu.VMEM((more + 1, block, loads), BF),
        ],
    )(late_list, flags, matrix, picked, total, late, late_core, far, far_in, near)
    return jnp.transpose(result, (2, 0, 1, 3)).reshape(per, block, loads)[None]


def solution(mesh):
    placed = (
        P("sub", "blk", None, None),
        P("sub", "blk", None, None, None),
        P("sub", "blk", None),
        P("sub", "blk", None, None),
        P("sub", "blk", None, None),
        P("sub", "blk", None, None),
        P("sub", None, None, None),
        P(),
    )
    return jax.shard_map(
        functools.partial(shards, mesh.shape["sub"], mesh.shape["blk"]),
        mesh=mesh,
        in_specs=placed,
        out_specs=P("sub", "blk", None, None),
        check_vma=False,
    )
```

profile of v0, /device:TPU:0, one launch (start us, length us, event | category | flops | bytes accessed | tf_op | source)
XLA Modules:
  0.0 41.3 jit_solution(5352266889851294649)
XLA Ops:
  0.1 1.0 %copy-done.1 = bf16[1,2,375,192]{2,3,1,0:T(8,128)(2,1)S(1)} copy-done((bf16[1,2,375,192]{2,3,1,0:T(8,128)(2,1)S(1)}, bf16[1,2,375,192]{2,3,1,0:T(8,128)(2,1)}, u32[]{:S(2)}) %copy-start.1) | copy-done | bytes 288024
  1.0 2.4 %shard_map.82 = (bf16[2,192,375]{2,1,0:T(8,128)(2,1)S(1)}, f32[3,192,192]{2,1,0:T(8,128)S(1)}, bf16[2,375,256]{2,1,0:T(8,128)(2,1)S(1)}, f32[2,192,128]{2,1,0:T(8,128)S(1)}, f32[2,192,128]{2,1,0:T(8,128)S(1)}) custom-call(s32[3]{0:T(128)S(1)} %add_convert_fusion.flags_ref, f32[375,2,2,128]{3,2,1,0:T(2,128)} %bitcast.53, bf16[2,192,375]{2,1,0:T(8,128)(2,1)S(1)} %bitcast.47, ...), custom_call_target="tpu_custom_call" | custom-call | flops 73728000 | tf_op jit(solution)/shard_map/pallas_call | solution.py:314
  4.0 1.1 %collective-permute-done.got_ref = f32[2,192,128]{2,1,0:T(8,128)S(1)} collective-permute-done((f32[2,192,128]{2,1,0:T(8,128)S(1)}, f32[2,192,128]{2,1,0:T(8,128)S(1)}, u32[]{:S(2)}, u32[]{:S(2)}) %collective-permute-start) | collective-permute-done | bytes 196640 | tf_op jit(solution)/shard_map/ppermute | solution.py:24
  5.1 3.9 %collective-permute-start.3 = (bf16[192,128]{1,0:T(8,128)(2,1)S(1)}, bf16[192,128]{1,0:T(8,128)(2,1)S(1)}, u32[]{:S(2)}, u32[]{:S(2)}) collective-permute-start(bf16[192,128]{1,0:T(8,128)(2,1)S(1)} %get-tuple-element.79), channel_id=1, source_target_pairs={{0,6},{1,7},{2,4},{3,5},{4,2},{5,3},{6,0},{7,1},{8,14},{9,15},{10,... | collective-permute-start | bytes 147464 | tf_op jit(solution)/shard_map/ppermute | solution.py:24
  9.6 1.1 %copy-done.3 = bf16[1,2,375,375]{3,1,2,0:T(2,128)(2,1)S(1)} copy-done((bf16[1,2,375,375]{3,1,2,0:T(2,128)(2,1)S(1)}, bf16[1,2,375,375]{3,1,2,0:T(2,128)(2,1)}, u32[]{:S(2)}) %copy-start.3) | copy-done | bytes 562524
  10.6 1.5 %shard_map.83 = (f32[375,256]{1,0:T(8,128)S(1)}, f32[375,256]{1,0:T(8,128)S(1)}, bf16[375,448]{1,0:T(8,128)(2,1)S(1)}, bf16[375,448]{1,0:T(8,128)(2,1)S(1)}) custom-call(s32[3]{0:T(128)S(1)} %add_convert_fusion.flags_ref, bf16[2,375,256]{2,1,0:T(8,128)(2,1)S(1)} %get-tuple-element.45.scaled_ref, bf16[375,2,375]{2,1,0:T(2,128)(2,1)S(1)} %bitcast.51, ...), custom_call_target="tpu_custom_call" | custom-call | flops 99999997952 | tf_op jit(solution)/shard_map/pallas_call | solution.py:327
  12.2 0.9 %collective-permute-done.2 = bf16[192,128]{1,0:T(8,128)(2,1)S(1)} collective-permute-done((bf16[192,128]{1,0:T(8,128)(2,1)S(1)}, bf16[192,128]{1,0:T(8,128)(2,1)S(1)}, u32[]{:S(2)}, u32[]{:S(2)}) %collective-permute-start.2) | collective-permute-done | bytes 49184 | tf_op jit(solution)/shard_map/ppermute | solution.py:24
  13.6 0.6 %shard_map.84 = (f32[192,128]{1,0:T(8,128)S(1)}, f32[192,128]{1,0:T(8,128)S(1)}, f32[192,128]{1,0:T(8,128)S(1)}, bf16[192,128]{1,0:T(8,128)(2,1)S(1)}, bf16[192,128]{1,0:T(8,128)(2,1)S(1)}) custom-call(f32[2,192,128]{2,1,0:T(8,128)S(1)} %get-tuple-element.42.keep_ref, f32[2,192,128]{2,1,0:T(8,128)S(1)} %collective-permute-done.got_ref, ...), custom_call_target="tpu_custom_call" | custom-call | flops 28311552 | bytes 294912 | tf_op jit(solution)/shard_map/pallas_call | solution.py:345
  14.3 1.6 %collective-permute-start.4 = (bf16[192,128]{1,0:T(8,128)(2,1)S(1)}, bf16[192,128]{1,0:T(8,128)(2,1)S(1)}, u32[]{:S(2)}, u32[]{:S(2)}) collective-permute-start(bf16[192,128]{1,0:T(8,128)(2,1)S(1)} %get-tuple-element.52), channel_id=1, source_target_pairs={{0,8},{1,9},{2,10},{3,11},{4,12},{5,13},{6,14},{7,15},{8,0},{9,1},... | collective-permute-start | bytes 147464 | tf_op jit(solution)/shard_map/ppermute | solution.py:24
  16.8 1.6 %collective-permute-start.7 = (bf16[375,448]{1,0:T(8,128)(2,1)S(1)}, bf16[375,448]{1,0:T(8,128)(2,1)S(1)}, u32[]{:S(2)}, u32[]{:S(2)}) collective-permute-start(bf16[375,448]{1,0:T(8,128)(2,1)S(1)} %shard_map.87), channel_id=1, source_target_pairs={{0,4},{1,5},{2,6},{3,7},{4,0},{5,1},{6,2},{7,3},{8,12},{9,13},{10,... | collective-permute-start | bytes 1008008 | tf_op jit(solution)/shard_map/ppermute | solution.py:24
  18.7 2.7 %collective-permute-start.5 = (bf16[192,128]{1,0:T(8,128)(2,1)S(1)}, bf16[192,128]{1,0:T(8,128)(2,1)S(1)}, u32[]{:S(2)}, u32[]{:S(2)}) collective-permute-start(bf16[192,128]{1,0:T(8,128)(2,1)S(1)} %get-tuple-element.54), channel_id=1, source_target_pairs={{0,16},{1,17},{2,18},{3,19},{4,20},{5,21},{6,22},{7,23},{8,24},{9,... | collective-permute-start | bytes 147464 | tf_op jit(solution)/shard_map/ppermute | solution.py:24
  21.4 2.8 %constant_dynamic-slice_fusion = bf16[1,1,16,375,375]{4,2,3,1,0:T(8,128)(2,1)S(1)} fusion(bf16[1,2,16,375,375]{4,2,3,1,0:T(8,128)(2,1)} %param.9, s32[]{:T(128)S(6)} %select_n.88), kind=kLoop, calls=%fused_computation.30 | loop fusion | bytes 9000004 | tf_op jit(solution)/shard_map/jit(dynamic_index_in_dim)/dynamic_slice | solution.py:383
  24.2 1.0 %copy.11 = bf16[1,1,16,375,375]{4,3,2,1,0:T(8,128)(2,1)S(1)} copy(bf16[1,1,16,375,375]{4,2,3,1,0:T(8,128)(2,1)S(1)} %constant_dynamic-slice_fusion) | data formatting | bytes 9000000 | tf_op jit(solution)/shard_map/jit(dynamic_index_in_dim)/dynamic_slice | solution.py:383
  25.2 1.0 %shard_map.86 = bf16[2,192,128]{2,1,0:T(8,128)(2,1)S(1)} custom-call(f32[192,128]{1,0:T(8,128)S(1)} %get-tuple-element.53.own_ref, bf16[192,128]{1,0:T(8,128)(2,1)S(1)} %collective-permute-done.5.got_ref, f32[3,192,192]{2,1,0:T(8,128)S(1)} %get-tuple-element.50.map_ref, f32[192,192]{1,0:T(8,128)S(1)} %copy-done.2, ...), custom_call_target="tpu_custom_call" | custom-call | flops 56623104 | bytes 737280 | tf_op jit(solution)/shard_map/pallas_call | solution.py:374
  26.3 0.7 %collective-permute-done.8 = bf16[375,448]{1,0:T(8,128)(2,1)S(1)} collective-permute-done((bf16[375,448]{1,0:T(8,128)(2,1)S(1)}, bf16[375,448]{1,0:T(8,128)(2,1)S(1)}, u32[]{:S(2)}, u32[]{:S(2)}) %collective-permute-start.8) | collective-permute-done | bytes 336032 | tf_op jit(solution)/shard_map/ppermute | solution.py:24
  26.9 0.7 %collective-permute-done.7.near_in_ref = bf16[375,448]{1,0:T(8,128)(2,1)S(1)} collective-permute-done((bf16[375,448]{1,0:T(8,128)(2,1)S(1)}, bf16[375,448]{1,0:T(8,128)(2,1)S(1)}, u32[]{:S(2)}, u32[]{:S(2)}) %collective-permute-start.7) | collective-permute-done | bytes 336032 | tf_op jit(solution)/shard_map/ppermute | solution.py:24
  27.6 1.3 %collective-permute-done.9 = bf16[2,192,128]{2,1,0:T(8,128)(2,1)S(1)} collective-permute-done((bf16[2,192,128]{2,1,0:T(8,128)(2,1)S(1)}, bf16[2,192,128]{2,1,0:T(8,128)(2,1)S(1)}, u32[]{:S(2)}, u32[]{:S(2)}) %collective-permute-start.9) | collective-permute-done | bytes 98336 | tf_op jit(solution)/shard_map/ppermute | solution.py:24
  29.3 0.8 %shard_map.89 = (f32[375,256]{1,0:T(8,128)S(1)}, bf16[375,256]{1,0:T(8,128)(2,1)S(1)}, bf16[3,375,256]{2,1,0:T(8,128)(2,1)S(1)}) custom-call(s32[3]{0:T(128)S(1)} %add_convert_fusion.flags_ref, bf16[2,192,256]{2,1,0:T(8,128)(2,1)S(1)} %pad_maximum_fusion.fields_ref, bf16[375,256]{1,0:T(8,128)(2,1)S(1)} %get-tuple-element.66.near_ref, ...), custom_call_target="tpu_custom_call" | custom-call | flops 99999997952 | bytes 2304000 | tf_op jit(solution)/shard_map/pallas_call | solution.py:404
  30.3 1.5 %collective-permute-start.11 = (bf16[375,256]{1,0:T(8,128)(2,1)S(1)}, bf16[375,256]{1,0:T(8,128)(2,1)S(1)}, u32[]{:S(2)}, u32[]{:S(2)}) collective-permute-start(bf16[375,256]{1,0:T(8,128)(2,1)S(1)} %get-tuple-element.66.near_ref), channel_id=1, source_target_pairs={{0,2},{1,3},{2,0},{3,1},{4,5},{5,4},{6,7},{7,6},{8,9},{9,8},{10,11... | collective-permute-start | bytes 576008 | tf_op jit(solution)/shard_map/ppermute | solution.py:24
  31.9 1.4 %shard_map.91.picked_ref = bf16[375,375]{1,0:T(8,128)(2,1)S(1)} custom-call(s32[3]{0:T(128)S(1)} %add_convert_fusion.flags_ref, bf16[375,2,375]{2,1,0:T(2,128)(2,1)S(1)} %bitcast.46), custom_call_target="tpu_custom_call" | custom-call | flops 1000 | tf_op jit(solution)/shard_map/pallas_call | solution.py:413
  33.3 2.8 %shard_map.90 = (f32[375,256]{1,0:T(8,128)S(1)}, s32[3,16]{1,0:T(4,128)S(1)}) custom-call(s32[16]{0:T(128)S(1)} %and_select_fusion.1.slots_ref, s32[3]{0:T(128)S(1)} %add_convert_fusion.flags_ref, bf16[16,375,375]{2,1,0:T(8,128)(2,1)S(1)} %bitcast.44, bf16[3,375,256]{2,1,0:T(8,128)(2,1)S(1)} %get-tuple-element.69.mine_ref, ...), custom_call_target="tpu_custom_call" | custom-call | flops 1000 | bytes 4500000 | tf_op jit(solution)/shard_map/pallas_call | solution.py:436
  36.2 1.2 %collective-permute-done.11 = bf16[375,256]{1,0:T(8,128)(2,1)S(1)} collective-permute-done((bf16[375,256]{1,0:T(8,128)(2,1)S(1)}, bf16[375,256]{1,0:T(8,128)(2,1)S(1)}, u32[]{:S(2)}, u32[]{:S(2)}) %collective-permute-start.11) | collective-permute-done | bytes 192032 | tf_op jit(solution)/shard_map/ppermute | solution.py:24
  37.4 1.4 %collective-permute-done.12.late_core_ref = bf16[1,375,256]{2,1,0:T(8,128)(2,1)S(1)} collective-permute-done((bf16[1,375,256]{2,1,0:T(8,128)(2,1)S(1)}, bf16[1,375,256]{2,1,0:T(8,128)(2,1)S(1)}, u32[]{:S(2)}, u32[]{:S(2)}) %collective-permute-start.12) | collective-permute-done | bytes 192032 | tf_op jit(solution)/shard_map/ppermute | solution.py:24
  38.8 2.5 %shard_map.92 = f32[375,2,2,128]{3,2,1,0:T(2,128)} custom-call(s32[3,16]{1,0:T(4,128)S(1)} %get-tuple-element.70.list_ref, s32[3]{0:T(128)S(1)} %add_convert_fusion.flags_ref, bf16[16,375,375]{2,1,0:T(8,128)(2,1)S(1)} %bitcast.45, bf16[375,375]{1,0:T(8,128)(2,1)S(1)} %shard_map.91.picked_ref, f32[375,256]{1,0:T(8,128)S(1)} %get-tuple-element.74.total_ref, ...), custom_call_target="tpu_custom_call" | custom-call | flops 72000000 | bytes 1536000 | tf_op jit(solution)/shard_map/pallas_call | solution.py:447
  (39 shorter events, 3.8 us)
Async XLA Ops:
  0.1 1.0 %copy-start.1 = (bf16[1,2,375,192]{2,3,1,0:T(8,128)(2,1)S(1)}, bf16[1,2,375,192]{2,3,1,0:T(8,128)(2,1)}, u32[]{:S(2)}) copy-start(bf16[1,2,375,192]{2,3,1,0:T(8,128)(2,1)} %param.13) | copy-start | bytes 864004
  3.4 1.6 %collective-permute-start = (f32[2,192,128]{2,1,0:T(8,128)S(1)}, f32[2,192,128]{2,1,0:T(8,128)S(1)}, u32[]{:S(2)}, u32[]{:S(2)}) collective-permute-start(f32[2,192,128]{2,1,0:T(8,128)S(1)} %get-tuple-element.43), channel_id=1, source_target_pairs={{0,1},{1,0},{2,3},{3,2},{4,5},{5,4},{6,7},{7,6},{8,9},{9,8},{10,11... | collective-permute-start | bytes 589832 | tf_op jit(solution)/shard_map/ppermute | solution.py:24
  5.1 7.1 %collective-permute-start.3 = (bf16[192,128]{1,0:T(8,128)(2,1)S(1)}, bf16[192,128]{1,0:T(8,128)(2,1)S(1)}, u32[]{:S(2)}, u32[]{:S(2)}) collective-permute-start(bf16[192,128]{1,0:T(8,128)(2,1)S(1)} %get-tuple-element.79), channel_id=1, source_target_pairs={{0,6},{1,7},{2,4},{3,5},{4,2},{5,3},{6,0},{7,1},{8,14},{9,15},{10,... | collective-permute-start | bytes 147464 | tf_op jit(solution)/shard_map/ppermute | solution.py:24
  8.9 4.1 %collective-permute-start.2 = (bf16[192,128]{1,0:T(8,128)(2,1)S(1)}, bf16[192,128]{1,0:T(8,128)(2,1)S(1)}, u32[]{:S(2)}, u32[]{:S(2)}) collective-permute-start(bf16[192,128]{1,0:T(8,128)(2,1)S(1)} %get-tuple-element.79), channel_id=1, source_target_pairs={{0,4},{1,5},{2,6},{3,7},{4,0},{5,1},{6,2},{7,3},{8,12},{9,13},{10,... | collective-permute-start | bytes 147464 | tf_op jit(solution)/shard_map/ppermute | solution.py:24
  9.5 4.1 %collective-permute-start.1 = (bf16[192,128]{1,0:T(8,128)(2,1)S(1)}, bf16[192,128]{1,0:T(8,128)(2,1)S(1)}, u32[]{:S(2)}, u32[]{:S(2)}) collective-permute-start(bf16[192,128]{1,0:T(8,128)(2,1)S(1)} %get-tuple-element.80), channel_id=1, source_target_pairs={{0,2},{1,3},{2,0},{3,1},{4,6},{5,7},{6,4},{7,5},{8,10},{9,11},{10,... | collective-permute-start | bytes 147464 | tf_op jit(solution)/shard_map/ppermute | solution.py:24
  9.6 1.1 %copy-start.3 = (bf16[1,2,375,375]{3,1,2,0:T(2,128)(2,1)S(1)}, bf16[1,2,375,375]{3,1,2,0:T(2,128)(2,1)}, u32[]{:S(2)}) copy-start(bf16[1,2,375,375]{3,1,2,0:T(2,128)(2,1)} %param.11) | copy-start | bytes 1687504
  12.1 2.0 %copy-start.4 = (f32[375,256]{1,0:T(8,128)}, f32[375,256]{1,0:T(8,128)S(1)}, u32[]{:S(2)}) copy-start(f32[375,256]{1,0:T(8,128)S(1)} %get-tuple-element.68.far_fix_ref) | copy-start | bytes 1152004
  14.2 2.3 %collective-permute-start.6 = (bf16[192,128]{1,0:T(8,128)(2,1)S(1)}, bf16[192,128]{1,0:T(8,128)(2,1)S(1)}, u32[]{:S(2)}, u32[]{:S(2)}) collective-permute-start(bf16[192,128]{1,0:T(8,128)(2,1)S(1)} %get-tuple-element.58), channel_id=1, source_target_pairs={{0,1},{1,0},{2,3},{3,2},{4,5},{5,4},{6,7},{7,6},{8,9},{9,8},{10,11... | collective-permute-start | bytes 147464 | tf_op jit(solution)/shard_map/ppermute | solution.py:24
  14.3 4.2 %collective-permute-start.4 = (bf16[192,128]{1,0:T(8,128)(2,1)S(1)}, bf16[192,128]{1,0:T(8,128)(2,1)S(1)}, u32[]{:S(2)}, u32[]{:S(2)}) collective-permute-start(bf16[192,128]{1,0:T(8,128)(2,1)S(1)} %get-tuple-element.52), channel_id=1, source_target_pairs={{0,8},{1,9},{2,10},{3,11},{4,12},{5,13},{6,14},{7,15},{8,0},{9,1},... | collective-permute-start | bytes 147464 | tf_op jit(solution)/shard_map/ppermute | solution.py:24
  15.9 11.0 %collective-permute-start.8 = (bf16[375,448]{1,0:T(8,128)(2,1)S(1)}, bf16[375,448]{1,0:T(8,128)(2,1)S(1)}, u32[]{:S(2)}, u32[]{:S(2)}) collective-permute-start(bf16[375,448]{1,0:T(8,128)(2,1)S(1)} %get-tuple-element.61.far_ref), channel_id=1, source_target_pairs={{0,2},{1,3},{2,0},{3,1},{4,6},{5,7},{6,4},{7,5},{8,10},{9,11},{10,... | collective-permute-start | bytes 1008008 | tf_op jit(solution)/shard_map/ppermute | solution.py:24
  16.8 10.8 %collective-permute-start.7 = (bf16[375,448]{1,0:T(8,128)(2,1)S(1)}, bf16[375,448]{1,0:T(8,128)(2,1)S(1)}, u32[]{:S(2)}, u32[]{:S(2)}) collective-permute-start(bf16[375,448]{1,0:T(8,128)(2,1)S(1)} %shard_map.87), channel_id=1, source_target_pairs={{0,4},{1,5},{2,6},{3,7},{4,0},{5,1},{6,2},{7,3},{8,12},{9,13},{10,... | collective-permute-start | bytes 1008008 | tf_op jit(solution)/shard_map/ppermute | solution.py:24
  18.7 6.5 %collective-permute-start.5 = (bf16[192,128]{1,0:T(8,128)(2,1)S(1)}, bf16[192,128]{1,0:T(8,128)(2,1)S(1)}, u32[]{:S(2)}, u32[]{:S(2)}) collective-permute-start(bf16[192,128]{1,0:T(8,128)(2,1)S(1)} %get-tuple-element.54), channel_id=1, source_target_pairs={{0,16},{1,17},{2,18},{3,19},{4,20},{5,21},{6,22},{7,23},{8,24},{9,... | collective-permute-start | bytes 147464 | tf_op jit(solution)/shard_map/ppermute | solution.py:24
  24.1 1.1 %copy-start.2 = (f32[192,192]{1,0:T(8,128)S(1)}, f32[192,192]{1,0:T(8,128)}, u32[]{:S(2)}) copy-start(f32[192,192]{1,0:T(8,128)} %root_ref.1) | copy-start | bytes 442372
  24.1 5.1 %copy-start.5 = (f32[375,256]{1,0:T(8,128)S(1)}, f32[375,256]{1,0:T(8,128)}, u32[]{:S(2)}) copy-start(f32[375,256]{1,0:T(8,128)} %copy-done.4) | copy-start | bytes 1152004
  27.6 1.3 %collective-permute-start.9 = (bf16[2,192,128]{2,1,0:T(8,128)(2,1)S(1)}, bf16[2,192,128]{2,1,0:T(8,128)(2,1)S(1)}, u32[]{:S(2)}, u32[]{:S(2)}) collective-permute-start(bf16[2,192,128]{2,1,0:T(8,128)(2,1)S(1)} %shard_map.86), channel_id=1, source_target_pairs={{0,1},{1,0},{2,3},{3,2},{4,5},{5,4},{6,7},{7,6},{8,9},{9,8},{10,11... | collective-permute-start | bytes 294920 | tf_op jit(solution)/shard_map/ppermute | solution.py:24
  29.2 2.5 %copy-start.6 = (s32[1,2,16]{2,1,0:T(2,128)S(1)}, s32[1,2,16]{2,1,0:T(2,128)}, u32[]{:S(2)}) copy-start(s32[1,2,16]{2,1,0:T(2,128)} %param.10) | copy-start | bytes 388
  29.2 2.7 %copy-start = (bf16[1,2,375,375]{3,1,2,0:T(2,128)(2,1)S(1)}, bf16[1,2,375,375]{3,1,2,0:T(2,128)(2,1)}, u32[]{:S(2)}) copy-start(bf16[1,2,375,375]{3,1,2,0:T(2,128)(2,1)} %param.12) | copy-start | bytes 1687504
  30.1 3.2 %collective-permute-start.10 = (bf16[3,375,256]{2,1,0:T(8,128)(2,1)S(1)}, bf16[3,375,256]{2,1,0:T(8,128)(2,1)S(1)}, u32[]{:S(2)}, u32[]{:S(2)}) collective-permute-start(bf16[3,375,256]{2,1,0:T(8,128)(2,1)S(1)} %get-tuple-element.69.mine_ref), channel_id=1, source_target_pairs={{0,1},{1,0},{2,3},{3,2},{4,5},{5,4},{6,7},{7,6},{8,9},{9,8},{10,11... | collective-permute-start | bytes 1728008 | tf_op jit(solution)/shard_map/ppermute | solution.py:24
  30.3 7.1 %collective-permute-start.11 = (bf16[375,256]{1,0:T(8,128)(2,1)S(1)}, bf16[375,256]{1,0:T(8,128)(2,1)S(1)}, u32[]{:S(2)}, u32[]{:S(2)}) collective-permute-start(bf16[375,256]{1,0:T(8,128)(2,1)S(1)} %get-tuple-element.66.near_ref), channel_id=1, source_target_pairs={{0,2},{1,3},{2,0},{3,1},{4,5},{5,4},{6,7},{7,6},{8,9},{9,8},{10,11... | collective-permute-start | bytes 576008 | tf_op jit(solution)/shard_map/ppermute | solution.py:24
  31.8 5.6 %collective-permute-start.13 = (bf16[375,256]{1,0:T(8,128)(2,1)S(1)}, bf16[375,256]{1,0:T(8,128)(2,1)S(1)}, u32[]{:S(2)}, u32[]{:S(2)}) collective-permute-start(bf16[375,256]{1,0:T(8,128)(2,1)S(1)} %get-tuple-element.77), channel_id=1, source_target_pairs={{0,1},{1,0},{2,3},{3,2},{4,8},{5,9},{6,10},{7,11},{8,4},{9,5},{10,... | collective-permute-start | bytes 576008 | tf_op jit(solution)/shard_map/ppermute | solution.py:24
  37.4 1.4 %collective-permute-start.12 = (bf16[1,375,256]{2,1,0:T(8,128)(2,1)S(1)}, bf16[1,375,256]{2,1,0:T(8,128)(2,1)S(1)}, u32[]{:S(2)}, u32[]{:S(2)}) collective-permute-start(bf16[1,375,256]{2,1,0:T(8,128)(2,1)S(1)} %bitcast.48), channel_id=1, source_target_pairs={{0,1},{1,0},{2,3},{3,2},{4,5},{5,4},{6,7},{7,6},{8,9},{9,8},{10,11... | collective-permute-start | bytes 576008 | tf_op jit(solution)/shard_map/ppermute | solution.py:24
where the time goes:
time: 41.5 us; the launch traced here: 41.3 us
  Pallas kernels  13.9 us (33%)
  starting transfers between devices  13.4 us (32%)
  waiting for transfers between devices  7.79 us (19%)
  local copies, waits for them, and re-layouts  5.84 us (14%)
    ppermute x14, starting transfers between devices, route(): return lax.ppermute(x, ('sub', 'blk'), pairs)  13.4 us
    ppermute x14, waiting for transfers between devices, route(): return lax.ppermute(x, ('sub', 'blk'), pairs)  7.79 us
    dynamic_slice x2, local copies, waits for them, and re-layouts, shards(): lax.dynamic_index_in_dim(stiffness[0], after(far_id, own_bf), 0, False)  3.79 us
    pallas_call x1, Pallas kernels, shards(): call(functools.partial(couple_kernel, more), (shape((block, loads), F32),...  2.84 us
    pallas_call x1, Pallas kernels, shards(): call(finish_kernel, shape((block, parts, per, lanes), F32), [SMEM, SMEM]...  2.54 us
    pallas_call x1, Pallas kernels, shards(): call(start_kernel, tuple((shape(x.shape, x.dtype) for x in given)) + (sha...  2.39 us
    unnamed x14, local copies, waits for them, and re-layouts  2.05 us
    pallas_call x1, Pallas kernels, shards(): call(local_kernel, (shape((block, loads), F32),) * 2 + (shape((block, loa...  1.48 us
  transfers between devices with their start and end apart: 14, of which 8 were waited for; matrix products, arithmetic and copies ran while one was open for 9% of the time, Pallas kernels for 18%

commit v1 on v0

--- a/solution.py
+++ b/solution.py
@@ -97,14 +97,20 @@
         copy.wait()
 
 
-def local_kernel(flags_ref, scaled_ref, inverse_hbm, modes_ref, near_ref, far_ref, near_out, far_out, inverse_ref, rows_ref, sem):
+def local_kernel(flags_ref, scaled_ref, inverse_hbm, modes_ref, map_ref, near_ref, far_ref, near_modes, far_modes, far_out, mapped_out, inverse_ref, rows_ref, sem):
     copy = pltpu.make_async_copy(inverse_hbm, inverse_ref, sem)
     copy.start()
     loads = scaled_ref.shape[-1]
     is_even = flags_ref[0] > 0
     low_modes, high_modes = (modes_ref[j].T for j in range(2))
-    near_out[:, loads:] = jnp.where(is_even, high_modes, low_modes)
-    far_out[:, loads:] = jnp.where(is_even, low_modes, high_modes)
+    near_modes[...] = jnp.where(is_even, high_modes, low_modes)
+    far_modes[...] = jnp.where(is_even, low_modes, high_modes)
+    far_out[loads:] = jnp.where(is_even, modes_ref[0], modes_ref[1])
+    turned = map_ref[0].T
+    high = turned.astype(BF)
+    low = (turned - high.astype(F32)).astype(BF)
+    near = jnp.where(is_even, modes_ref[1], modes_ref[0])
+    mapped_out[...] = (bdot(high, near) + bdot(low, near)).astype(BF)
     copy.wait()
     rows, per, columns = inverse_ref.shape
     inverse = inverse_ref[...].reshape(rows * per, columns)
@@ -118,8 +124,7 @@
         near, far = jnp.where(is_even, high, low), jnp.where(is_even, low, high)
         near_ref[:, here] = near
         far_ref[:, here] = far
-        near_out[:, here] = near.astype(BF)
-        far_out[:, here] = far.astype(BF)
+        far_out[here] = far.astype(BF).T
 
 
 def pair_kernel(keep_ref, got_ref, same_ref, cross_ref, map_ref, coarse_ref, pair_ref, own_ref, sent_ref, share_ref):
@@ -137,13 +142,16 @@
     share_ref[...] = coarse.astype(BF)
 
 
-def offer_kernel(coarse_ref, near_ref, near_fix_ref, map_ref, out_ref):
+def offer_kernel(coarse_ref, near_modes, mapped_ref, near_fix_ref, out_ref):
     loads = near_fix_ref.shape[-1]
-    modes = near_ref[:, loads:]
-    out_ref[:, :loads] = (near_fix_ref[...] + bdot(modes, coarse_ref[...])).astype(BF)
-    high = map_ref[0].astype(BF)
-    low = (map_ref[0] - high.astype(F32)).astype(BF)
-    out_ref[:, loads:] = (bdot(modes, high) + bdot(modes, low)).astype(BF)
+    out_ref[:loads] = (near_fix_ref[...] + bdot(near_modes[...], coarse_ref[...])).astype(BF).T
+    out_ref[loads:] = mapped_ref[...]
+
+
+def turn_kernel(near_ref, far_ref, near_out, far_out):
+    near_out[...] = near_ref[...].T
+    for i in range(far_ref.shape[0]):
+        far_out[i] = far_ref[i].T
 
 
 def level_kernel(level, own_ref, got_ref, map_ref, value_ref, next_ref, sent_ref):
@@ -163,20 +171,20 @@
     fields_ref[1] = field.astype(BF)
 
 
-def near_kernel(fields_ref, near_ref, near_in_ref, near_fix_ref, near_out, near_bf):
+def near_kernel(fields_ref, near_modes, near_in_ref, near_fix_ref, near_out, near_bf):
     loads = near_fix_ref.shape[-1]
-    own = near_fix_ref[...] + bdot(near_ref[:, loads:], fields_ref[0])
+    own = near_fix_ref[...] + bdot(near_modes[...], fields_ref[0])
     other = near_in_ref[:, :loads].astype(F32) + bdot(near_in_ref[:, loads:], fields_ref[1])
     near = 0.5 * own + 0.5 * other
     near_out[...] = near
     near_bf[...] = near.astype(BF)
 
 
-def far_kernel(flags_ref, fields_ref, near_ref, far_ref, far_in_ref, far_fix_ref, far_out, far_bf, mine_bf):
+def far_kernel(flags_ref, fields_ref, near_ref, far_modes, far_in_ref, far_fix_ref, far_out, far_bf, mine_bf):
     loads = far_fix_ref.shape[-1]
     field = fields_ref[0]
     scale = jnp.where(flags_ref[1] > 0, 1.0, 0.5).astype(F32)
-    far = (far_fix_ref[...] + bdot(far_ref[:, loads:], field)) * scale
+    far = (far_fix_ref[...] + bdot(far_modes[...], field)) * scale
     far_out[...] = far
     far_bf[...] = far.astype(BF)
     mine_bf[0] = far.astype(BF)
@@ -324,10 +332,12 @@
     )(flags, laid, *given)
     got = swap(sent, blk=1)
     neumann = turned(neumann_inv)
-    near_fix, far_fix, to_sibling, to_far = call(
+    near_fix, far_fix, near_modes, far_modes, to_far, mapped_modes = call(
         local_kernel,
-        (shape((block, loads), F32),) * 2 + (shape((block, loads + width), BF),) * 2,
-        [SMEM, VMEM, HBM, VMEM],
+        (shape((block, loads), F32),) * 2
+        + (shape((block, width), BF),) * 2
+        + (shape((loads + width, block), BF), shape((width, block), BF)),
+        [SMEM, VMEM, HBM, VMEM, VMEM],
         large,
         0,
         [
@@ -336,12 +346,12 @@
             pltpu.SemaphoreType.DMA(()),
         ],
         16,
-    )(flags, after(scaled, got), neumann, modes)
+    )(flags, after(scaled, got), neumann, modes, maps)
     half_bf, mapped_bf = (keep[0] + got[0]).astype(BF), (keep[1] + got[1]).astype(BF)
 
     same = jnp.stack([swap(half_bf, blk=d) for d in others])
     cross = jnp.stack([swap(mapped_bf, sub=1, blk=d) for d in (0,) + tuple(others)])
-    cross, to_sibling, to_far = lax.optimization_barrier((cross, to_sibling, to_far))
+    cross, near_fix, to_far = lax.optimization_barrier((cross, near_fix, to_far))
     coarse, value, own, own_bf, share = call(
         pair_kernel,
         (shape(half_shape, F32),) * 3
@@ -353,11 +363,11 @@
     )(keep, got, same, cross, maps)
     offer = call(
         offer_kernel,
-        shape(to_sibling.shape, BF),
+        shape(to_far.shape, BF),
         [VMEM] * 4,
         3 * 10**9,
         0,
-    )(joined(share), to_sibling, near_fix, maps)
+    )(joined(share), near_modes, mapped_modes, near_fix)
     from_sibling = swap(offer, sub=1)
     from_others = jnp.stack([swap(to_far, blk=d) for d in others])
     values = [value]
@@ -384,7 +394,14 @@
     fields, from_sibling, from_others, matrix = lax.optimization_barrier(
         (fields, from_sibling, from_others, matrix)
     )
-    fields = joined(fields)
+    from_sibling, from_others = call(
+        turn_kernel,
+        (shape((block, loads + width), BF), shape((len(others), block, loads + width), BF)),
+        [VMEM] * 2,
+        10**9,
+        0,
+    )(from_sibling, from_others)
+    fields, from_sibling, from_others = lax.optimization_barrier((joined(fields), from_sibling, from_others))
 
     count = 2 + len(others)
     face = 2 * block * width * loads
@@ -394,7 +411,7 @@
         [VMEM] * 4,
         2 * face,
         block * loads * 8,
-    )(fields, to_sibling, from_sibling, near_fix)
+    )(fields, near_modes, from_sibling, near_fix)
     late = jnp.stack(
         [
             go(near_bf, target=lambda s, b, d=d: (s, b ^ d) if s in (0, subs - 1) else (s, b ^ 1))
@@ -407,7 +424,7 @@
         [SMEM] + [VMEM] * 5,
         10**11,
         count * block * loads * 8,
-    )(flags, fields, near_bf, to_far, from_others, far_fix)
+    )(flags, fields, near_bf, far_modes, from_others, far_fix)
 
     core = swap(mine_bf, blk=1)
     picked = call(

time: 41.5 us -> 40.9 us (0.986)
  waiting for transfers between devices: 7.79 us -> 6.64 us
  Pallas kernels: 13.9 us -> 14.4 us
    ppermute x14, waiting for transfers between devices: 7.79 us -> 6.64 us  [route(): return lax.ppermute(x, ('sub', 'blk'), pairs)]
    pallas_call x2 -> x3, Pallas kernels: 1.8 us -> 2.27 us  [the longest x1 1.72 us: shards(): call(local_kernel, (shape((block, loads), F32),) * 2 + (shape((block, wid...]
  transfers between devices with their start and end apart: 14 -> 14, of which waited for: 8 -> 7; matrix products, arithmetic and copies ran while one was open for 9% -> 9% of each run, Pallas kernels for 18% -> 19%
where the time goes in v1:
time: 40.9 us; the launch traced here: 40.7 us
  Pallas kernels  14.4 us (35%)
  starting transfers between devices  13.4 us (33%)
  waiting for transfers between devices  6.64 us (16%)
  local copies, waits for them, and re-layouts  5.84 us (14%)
    ppermute x14, starting transfers between devices, route(): return lax.ppermute(x, ('sub', 'blk'), pairs)  13.4 us
    ppermute x14, waiting for transfers between devices, route(): return lax.ppermute(x, ('sub', 'blk'), pairs)  6.64 us
    dynamic_slice x2, local copies, waits for them, and re-layouts, shards(): lax.dynamic_index_in_dim(stiffness[0], after(far_id, own_bf), 0, False)  3.79 us
    pallas_call x1, Pallas kernels, shards(): call(functools.partial(couple_kernel, more), (shape((block, loads), F32),...  2.84 us
    pallas_call x1, Pallas kernels, shards(): call(finish_kernel, shape((block, parts, per, lanes), F32), [SMEM, SMEM]...  2.57 us
    pallas_call x1, Pallas kernels, shards(): call(start_kernel, tuple((shape(x.shape, x.dtype) for x in given)) + (sha...  2.39 us
    unnamed x14, local copies, waits for them, and re-layouts  2.05 us
    pallas_call x1, Pallas kernels, shards(): call(local_kernel, (shape((block, loads), F32),) * 2 + (shape((block, wid...  1.72 us
  transfers between devices with their start and end apart: 14, of which 7 were waited for; matrix products, arithmetic and copies ran while one was open for 9% of the time, Pallas kernels for 19%

profile of v1, /device:TPU:0, one launch (start us, length us, event | category | flops | bytes accessed | tf_op | source)
XLA Modules:
  0.0 40.7 jit_solution(7486858172918735447)
XLA Ops:
  0.1 1.0 %copy-done.1 = bf16[1,2,375,192]{2,3,1,0:T(8,128)(2,1)S(1)} copy-done((bf16[1,2,375,192]{2,3,1,0:T(8,128)(2,1)S(1)}, bf16[1,2,375,192]{2,3,1,0:T(8,128)(2,1)}, u32[]{:S(2)}) %copy-start.1) | copy-done | bytes 288024
  1.0 2.4 %shard_map.82 = (bf16[2,192,375]{2,1,0:T(8,128)(2,1)S(1)}, f32[3,192,192]{2,1,0:T(8,128)S(1)}, bf16[2,375,256]{2,1,0:T(8,128)(2,1)S(1)}, f32[2,192,128]{2,1,0:T(8,128)S(1)}, f32[2,192,128]{2,1,0:T(8,128)S(1)}) custom-call(s32[3]{0:T(128)S(1)} %add_convert_fusion.flags_ref, f32[375,2,2,128]{3,2,1,0:T(2,128)} %bitcast.53, bf16[2,192,375]{2,1,0:T(8,128)(2,1)S(1)} %bitcast.47, ...), custom_call_target="tpu_custom_call" | custom-call | flops 73728000 | tf_op jit(solution)/shard_map/pallas_call | solution.py:322
  4.0 1.1 %collective-permute-done.got_ref = f32[2,192,128]{2,1,0:T(8,128)S(1)} collective-permute-done((f32[2,192,128]{2,1,0:T(8,128)S(1)}, f32[2,192,128]{2,1,0:T(8,128)S(1)}, u32[]{:S(2)}, u32[]{:S(2)}) %collective-permute-start) | collective-permute-done | bytes 196640 | tf_op jit(solution)/shard_map/ppermute | solution.py:24
  5.1 3.9 %collective-permute-start.3 = (bf16[192,128]{1,0:T(8,128)(2,1)S(1)}, bf16[192,128]{1,0:T(8,128)(2,1)S(1)}, u32[]{:S(2)}, u32[]{:S(2)}) collective-permute-start(bf16[192,128]{1,0:T(8,128)(2,1)S(1)} %get-tuple-element.93), channel_id=1, source_target_pairs={{0,6},{1,7},{2,4},{3,5},{4,2},{5,3},{6,0},{7,1},{8,14},{9,15},{10,... | collective-permute-start | bytes 147464 | tf_op jit(solution)/shard_map/ppermute | solution.py:24
  8.9 0.5 %collective-permute-start.2 = (bf16[192,128]{1,0:T(8,128)(2,1)S(1)}, bf16[192,128]{1,0:T(8,128)(2,1)S(1)}, u32[]{:S(2)}, u32[]{:S(2)}) collective-permute-start(bf16[192,128]{1,0:T(8,128)(2,1)S(1)} %get-tuple-element.93), channel_id=1, source_target_pairs={{0,4},{1,5},{2,6},{3,7},{4,0},{5,1},{6,2},{7,3},{8,12},{9,13},{10,... | collective-permute-start | bytes 147464 | tf_op jit(solution)/shard_map/ppermute | solution.py:24
  9.6 1.1 %copy-done.3 = bf16[1,2,375,375]{3,1,2,0:T(2,128)(2,1)S(1)} copy-done((bf16[1,2,375,375]{3,1,2,0:T(2,128)(2,1)S(1)}, bf16[1,2,375,375]{3,1,2,0:T(2,128)(2,1)}, u32[]{:S(2)}) %copy-start.3) | copy-done | bytes 562524
  10.6 1.7 %shard_map.83 = (f32[375,256]{1,0:T(8,128)S(1)}, f32[375,256]{1,0:T(8,128)S(1)}, bf16[375,192]{1,0:T(8,128)(2,1)S(1)}, bf16[375,192]{1,0:T(8,128)(2,1)S(1)}, bf1...) custom-call(s32[3]{0:T(128)S(1)} %add_convert_fusion.flags_ref, ...), custom_call_target="tpu_custom_call" | custom-call | flops 99999997952 | tf_op jit(solution)/shard_map/pallas_call | solution.py:335
  12.4 0.6 %collective-permute-done.2 = bf16[192,128]{1,0:T(8,128)(2,1)S(1)} collective-permute-done((bf16[192,128]{1,0:T(8,128)(2,1)S(1)}, bf16[192,128]{1,0:T(8,128)(2,1)S(1)}, u32[]{:S(2)}, u32[]{:S(2)}) %collective-permute-start.2) | collective-permute-done | bytes 49184 | tf_op jit(solution)/shard_map/ppermute | solution.py:24
  13.6 0.6 %shard_map.84 = (f32[192,128]{1,0:T(8,128)S(1)}, f32[192,128]{1,0:T(8,128)S(1)}, f32[192,128]{1,0:T(8,128)S(1)}, bf16[192,128]{1,0:T(8,128)(2,1)S(1)}, bf16[192,128]{1,0:T(8,128)(2,1)S(1)}) custom-call(f32[2,192,128]{2,1,0:T(8,128)S(1)} %get-tuple-element.49.keep_ref, f32[2,192,128]{2,1,0:T(8,128)S(1)} %collective-permute-done.got_ref, ...), custom_call_target="tpu_custom_call" | custom-call | flops 28311552 | bytes 294912 | tf_op jit(solution)/shard_map/pallas_call | solution.py:355
  14.3 1.6 %collective-permute-start.4 = (bf16[192,128]{1,0:T(8,128)(2,1)S(1)}, bf16[192,128]{1,0:T(8,128)(2,1)S(1)}, u32[]{:S(2)}, u32[]{:S(2)}) collective-permute-start(bf16[192,128]{1,0:T(8,128)(2,1)S(1)} %get-tuple-element.59), channel_id=1, source_target_pairs={{0,8},{1,9},{2,10},{3,11},{4,12},{5,13},{6,14},{7,15},{8,0},{9,1},... | collective-permute-start | bytes 147464 | tf_op jit(solution)/shard_map/ppermute | solution.py:24
  15.9 0.8 %collective-permute-start.8 = (bf16[448,375]{1,0:T(8,128)(2,1)S(1)}, bf16[448,375]{1,0:T(8,128)(2,1)S(1)}, u32[]{:S(2)}, u32[]{:S(2)}) collective-permute-start(bf16[448,375]{1,0:T(8,128)(2,1)S(1)} %get-tuple-element.69), channel_id=1, source_target_pairs={{0,2},{1,3},{2,0},{3,1},{4,6},{5,7},{6,4},{7,5},{8,10},{9,11},{10,... | collective-permute-start | bytes 1008008 | tf_op jit(solution)/shard_map/ppermute | solution.py:24
  17.0 1.5 %collective-permute-start.7 = (bf16[448,375]{1,0:T(8,128)(2,1)S(1)}, bf16[448,375]{1,0:T(8,128)(2,1)S(1)}, u32[]{:S(2)}, u32[]{:S(2)}) collective-permute-start(bf16[448,375]{1,0:T(8,128)(2,1)S(1)} %shard_map.87), channel_id=1, source_target_pairs={{0,4},{1,5},{2,6},{3,7},{4,0},{5,1},{6,2},{7,3},{8,12},{9,13},{10,... | collective-permute-start | bytes 1008008 | tf_op jit(solution)/shard_map/ppermute | solution.py:24
  18.9 2.7 %collective-permute-start.5 = (bf16[192,128]{1,0:T(8,128)(2,1)S(1)}, bf16[192,128]{1,0:T(8,128)(2,1)S(1)}, u32[]{:S(2)}, u32[]{:S(2)}) collective-permute-start(bf16[192,128]{1,0:T(8,128)(2,1)S(1)} %get-tuple-element.61), channel_id=1, source_target_pairs={{0,16},{1,17},{2,18},{3,19},{4,20},{5,21},{6,22},{7,23},{8,24},{9,... | collective-permute-start | bytes 147464 | tf_op jit(solution)/shard_map/ppermute | solution.py:24
  21.6 2.8 %constant_dynamic-slice_fusion = bf16[1,1,16,375,375]{4,2,3,1,0:T(8,128)(2,1)S(1)} fusion(bf16[1,2,16,375,375]{4,2,3,1,0:T(8,128)(2,1)} %param.9, s32[]{:T(128)S(6)} %select_n.88), kind=kLoop, calls=%fused_computation.30 | loop fusion | bytes 9000004 | tf_op jit(solution)/shard_map/jit(dynamic_index_in_dim)/dynamic_slice | solution.py:393
  24.3 1.0 %copy.11 = bf16[1,1,16,375,375]{4,3,2,1,0:T(8,128)(2,1)S(1)} copy(bf16[1,1,16,375,375]{4,2,3,1,0:T(8,128)(2,1)S(1)} %constant_dynamic-slice_fusion) | data formatting | bytes 9000000 | tf_op jit(solution)/shard_map/jit(dynamic_index_in_dim)/dynamic_slice | solution.py:393
  25.4 1.0 %shard_map.86 = bf16[2,192,128]{2,1,0:T(8,128)(2,1)S(1)} custom-call(f32[192,128]{1,0:T(8,128)S(1)} %get-tuple-element.60.own_ref, bf16[192,128]{1,0:T(8,128)(2,1)S(1)} %collective-permute-done.5.got_ref, f32[3,192,192]{2,1,0:T(8,128)S(1)} %get-tuple-element.54.map_ref, f32[192,192]{1,0:T(8,128)S(1)} %copy-done.2, ...), custom_call_target="tpu_custom_call" | custom-call | flops 56623104 | bytes 737280 | tf_op jit(solution)/shard_map/pallas_call | solution.py:384
  27.2 1.0 %collective-permute-done.9 = bf16[2,192,128]{2,1,0:T(8,128)(2,1)S(1)} collective-permute-done((bf16[2,192,128]{2,1,0:T(8,128)(2,1)S(1)}, bf16[2,192,128]{2,1,0:T(8,128)(2,1)S(1)}, u32[]{:S(2)}, u32[]{:S(2)}) %collective-permute-start.9) | collective-permute-done | bytes 98336 | tf_op jit(solution)/shard_map/ppermute | solution.py:24
  28.6 0.8 %shard_map.90 = (f32[375,256]{1,0:T(8,128)S(1)}, bf16[375,256]{1,0:T(8,128)(2,1)S(1)}, bf16[3,375,256]{2,1,0:T(8,128)(2,1)S(1)}) custom-call(s32[3]{0:T(128)S(1)} %add_convert_fusion.flags_ref, bf16[2,192,256]{2,1,0:T(8,128)(2,1)S(1)} %pad_maximum_fusion.fields_ref, bf16[375,256]{1,0:T(8,128)(2,1)S(1)} %get-tuple-element.79.near_ref, ...), custom_call_target="tpu_custom_call" | custom-call | flops 99999997952 | bytes 2304000 | tf_op jit(solution)/shard_map/pallas_call | solution.py:421
  29.6 1.2 %collective-permute-start.11 = (bf16[375,256]{1,0:T(8,128)(2,1)S(1)}, bf16[375,256]{1,0:T(8,128)(2,1)S(1)}, u32[]{:S(2)}, u32[]{:S(2)}) collective-permute-start(bf16[375,256]{1,0:T(8,128)(2,1)S(1)} %get-tuple-element.79.near_ref), channel_id=1, source_target_pairs={{0,2},{1,3},{2,0},{3,1},{4,5},{5,4},{6,7},{7,6},{8,9},{9,8},{10,11... | collective-permute-start | bytes 576008 | tf_op jit(solution)/shard_map/ppermute | solution.py:24
  31.0 1.4 %shard_map.92.picked_ref = bf16[375,375]{1,0:T(8,128)(2,1)S(1)} custom-call(s32[3]{0:T(128)S(1)} %add_convert_fusion.flags_ref, bf16[375,2,375]{2,1,0:T(2,128)(2,1)S(1)} %bitcast.46), custom_call_target="tpu_custom_call" | custom-call | flops 1000 | tf_op jit(solution)/shard_map/pallas_call | solution.py:430
  32.4 2.8 %shard_map.91 = (f32[375,256]{1,0:T(8,128)S(1)}, s32[3,16]{1,0:T(4,128)S(1)}) custom-call(s32[16]{0:T(128)S(1)} %and_select_fusion.1.slots_ref, s32[3]{0:T(128)S(1)} %add_convert_fusion.flags_ref, bf16[16,375,375]{2,1,0:T(8,128)(2,1)S(1)} %bitcast.44, bf16[3,375,256]{2,1,0:T(8,128)(2,1)S(1)} %get-tuple-element.83.mine_ref, ...), custom_call_target="tpu_custom_call" | custom-call | flops 1000 | bytes 4500000 | tf_op jit(solution)/shard_map/pallas_call | solution.py:453
  35.3 1.4 %collective-permute-done.11 = bf16[375,256]{1,0:T(8,128)(2,1)S(1)} collective-permute-done((bf16[375,256]{1,0:T(8,128)(2,1)S(1)}, bf16[375,256]{1,0:T(8,128)(2,1)S(1)}, u32[]{:S(2)}, u32[]{:S(2)}) %collective-permute-start.11) | collective-permute-done | bytes 192032 | tf_op jit(solution)/shard_map/ppermute | solution.py:24
  36.7 1.4 %collective-permute-done.12.late_core_ref = bf16[1,375,256]{2,1,0:T(8,128)(2,1)S(1)} collective-permute-done((bf16[1,375,256]{2,1,0:T(8,128)(2,1)S(1)}, bf16[1,375,256]{2,1,0:T(8,128)(2,1)S(1)}, u32[]{:S(2)}, u32[]{:S(2)}) %collective-permute-start.12) | collective-permute-done | bytes 192032 | tf_op jit(solution)/shard_map/ppermute | solution.py:24
  38.1 2.6 %shard_map.93 = f32[375,2,2,128]{3,2,1,0:T(2,128)} custom-call(s32[3,16]{1,0:T(4,128)S(1)} %get-tuple-element.84.list_ref, s32[3]{0:T(128)S(1)} %add_convert_fusion.flags_ref, bf16[16,375,375]{2,1,0:T(8,128)(2,1)S(1)} %bitcast.45, bf16[375,375]{1,0:T(8,128)(2,1)S(1)} %shard_map.92.picked_ref, f32[375,256]{1,0:T(8,128)S(1)} %get-tuple-element.88.total_ref, ...), custom_call_target="tpu_custom_call" | custom-call | flops 72000000 | bytes 1536000 | tf_op jit(solution)/shard_map/pallas_call | solution.py:464
  (40 shorter events, 3.4 us)
Async XLA Ops:
  0.1 1.0 %copy-start.1 = (bf16[1,2,375,192]{2,3,1,0:T(8,128)(2,1)S(1)}, bf16[1,2,375,192]{2,3,1,0:T(8,128)(2,1)}, u32[]{:S(2)}) copy-start(bf16[1,2,375,192]{2,3,1,0:T(8,128)(2,1)} %param.13) | copy-start | bytes 864004
  3.4 1.6 %collective-permute-start = (f32[2,192,128]{2,1,0:T(8,128)S(1)}, f32[2,192,128]{2,1,0:T(8,128)S(1)}, u32[]{:S(2)}, u32[]{:S(2)}) collective-permute-start(f32[2,192,128]{2,1,0:T(8,128)S(1)} %get-tuple-element.50), channel_id=1, source_target_pairs={{0,1},{1,0},{2,3},{3,2},{4,5},{5,4},{6,7},{7,6},{8,9},{9,8},{10,11... | collective-permute-start | bytes 589832 | tf_op jit(solution)/shard_map/ppermute | solution.py:24
  5.1 7.3 %collective-permute-start.3 = (bf16[192,128]{1,0:T(8,128)(2,1)S(1)}, bf16[192,128]{1,0:T(8,128)(2,1)S(1)}, u32[]{:S(2)}, u32[]{:S(2)}) collective-permute-start(bf16[192,128]{1,0:T(8,128)(2,1)S(1)} %get-tuple-element.93), channel_id=1, source_target_pairs={{0,6},{1,7},{2,4},{3,5},{4,2},{5,3},{6,0},{7,1},{8,14},{9,15},{10,... | collective-permute-start | bytes 147464 | tf_op jit(solution)/shard_map/ppermute | solution.py:24
  8.9 4.1 %collective-permute-start.2 = (bf16[192,128]{1,0:T(8,128)(2,1)S(1)}, bf16[192,128]{1,0:T(8,128)(2,1)S(1)}, u32[]{:S(2)}, u32[]{:S(2)}) collective-permute-start(bf16[192,128]{1,0:T(8,128)(2,1)S(1)} %get-tuple-element.93), channel_id=1, source_target_pairs={{0,4},{1,5},{2,6},{3,7},{4,0},{5,1},{6,2},{7,3},{8,12},{9,13},{10,... | collective-permute-start | bytes 147464 | tf_op jit(solution)/shard_map/ppermute | solution.py:24
  9.5 4.1 %collective-permute-start.1 = (bf16[192,128]{1,0:T(8,128)(2,1)S(1)}, bf16[192,128]{1,0:T(8,128)(2,1)S(1)}, u32[]{:S(2)}, u32[]{:S(2)}) collective-permute-start(bf16[192,128]{1,0:T(8,128)(2,1)S(1)} %get-tuple-element.94), channel_id=1, source_target_pairs={{0,2},{1,3},{2,0},{3,1},{4,6},{5,7},{6,4},{7,5},{8,10},{9,11},{10,... | collective-permute-start | bytes 147464 | tf_op jit(solution)/shard_map/ppermute | solution.py:24
  9.6 1.1 %copy-start.3 = (bf16[1,2,375,375]{3,1,2,0:T(2,128)(2,1)S(1)}, bf16[1,2,375,375]{3,1,2,0:T(2,128)(2,1)}, u32[]{:S(2)}) copy-start(bf16[1,2,375,375]{3,1,2,0:T(2,128)(2,1)} %param.11) | copy-start | bytes 1687504
  12.4 1.8 %copy-start.4 = (bf16[375,192]{1,0:T(8,128)(2,1)}, bf16[375,192]{1,0:T(8,128)(2,1)S(1)}, u32[]{:S(2)}) copy-start(bf16[375,192]{1,0:T(8,128)(2,1)S(1)} %get-tuple-element.80.far_modes) | copy-start | bytes 432004
  14.2 2.5 %collective-permute-start.6 = (bf16[192,128]{1,0:T(8,128)(2,1)S(1)}, bf16[192,128]{1,0:T(8,128)(2,1)S(1)}, u32[]{:S(2)}, u32[]{:S(2)}) collective-permute-start(bf16[192,128]{1,0:T(8,128)(2,1)S(1)} %get-tuple-element.65), channel_id=1, source_target_pairs={{0,1},{1,0},{2,3},{3,2},{4,5},{5,4},{6,7},{7,6},{8,9},{9,8},{10,11... | collective-permute-start | bytes 147464 | tf_op jit(solution)/shard_map/ppermute | solution.py:24
  14.3 4.3 %collective-permute-start.4 = (bf16[192,128]{1,0:T(8,128)(2,1)S(1)}, bf16[192,128]{1,0:T(8,128)(2,1)S(1)}, u32[]{:S(2)}, u32[]{:S(2)}) collective-permute-start(bf16[192,128]{1,0:T(8,128)(2,1)S(1)} %get-tuple-element.59), channel_id=1, source_target_pairs={{0,8},{1,9},{2,10},{3,11},{4,12},{5,13},{6,14},{7,15},{8,0},{9,1},... | collective-permute-start | bytes 147464 | tf_op jit(solution)/shard_map/ppermute | solution.py:24
  15.9 10.5 %collective-permute-start.8 = (bf16[448,375]{1,0:T(8,128)(2,1)S(1)}, bf16[448,375]{1,0:T(8,128)(2,1)S(1)}, u32[]{:S(2)}, u32[]{:S(2)}) collective-permute-start(bf16[448,375]{1,0:T(8,128)(2,1)S(1)} %get-tuple-element.69), channel_id=1, source_target_pairs={{0,2},{1,3},{2,0},{3,1},{4,6},{5,7},{6,4},{7,5},{8,10},{9,11},{10,... | collective-permute-start | bytes 1008008 | tf_op jit(solution)/shard_map/ppermute | solution.py:24
  17.0 9.9 %collective-permute-start.7 = (bf16[448,375]{1,0:T(8,128)(2,1)S(1)}, bf16[448,375]{1,0:T(8,128)(2,1)S(1)}, u32[]{:S(2)}, u32[]{:S(2)}) collective-permute-start(bf16[448,375]{1,0:T(8,128)(2,1)S(1)} %shard_map.87), channel_id=1, source_target_pairs={{0,4},{1,5},{2,6},{3,7},{4,0},{5,1},{6,2},{7,3},{8,12},{9,13},{10,... | collective-permute-start | bytes 1008008 | tf_op jit(solution)/shard_map/ppermute | solution.py:24
  18.9 6.5 %collective-permute-start.5 = (bf16[192,128]{1,0:T(8,128)(2,1)S(1)}, bf16[192,128]{1,0:T(8,128)(2,1)S(1)}, u32[]{:S(2)}, u32[]{:S(2)}) collective-permute-start(bf16[192,128]{1,0:T(8,128)(2,1)S(1)} %get-tuple-element.61), channel_id=1, source_target_pairs={{0,16},{1,17},{2,18},{3,19},{4,20},{5,21},{6,22},{7,23},{8,24},{9,... | collective-permute-start | bytes 147464 | tf_op jit(solution)/shard_map/ppermute | solution.py:24
  24.3 1.1 %copy-start.2 = (f32[192,192]{1,0:T(8,128)S(1)}, f32[192,192]{1,0:T(8,128)}, u32[]{:S(2)}) copy-start(f32[192,192]{1,0:T(8,128)} %root_ref.1) | copy-start | bytes 442372
  25.4 3.2 %copy-start.5 = (bf16[375,192]{1,0:T(8,128)(2,1)S(1)}, bf16[375,192]{1,0:T(8,128)(2,1)}, u32[]{:S(2)}) copy-start(bf16[375,192]{1,0:T(8,128)(2,1)} %copy-done.4) | copy-start | bytes 432004
  26.9 1.3 %collective-permute-start.9 = (bf16[2,192,128]{2,1,0:T(8,128)(2,1)S(1)}, bf16[2,192,128]{2,1,0:T(8,128)(2,1)S(1)}, u32[]{:S(2)}, u32[]{:S(2)}) collective-permute-start(bf16[2,192,128]{2,1,0:T(8,128)(2,1)S(1)} %shard_map.86), channel_id=1, source_target_pairs={{0,1},{1,0},{2,3},{3,2},{4,5},{5,4},{6,7},{7,6},{8,9},{9,8},{10,11... | collective-permute-start | bytes 294920 | tf_op jit(solution)/shard_map/ppermute | solution.py:24
  28.6 2.3 %copy-start.6 = (s32[1,2,16]{2,1,0:T(2,128)S(1)}, s32[1,2,16]{2,1,0:T(2,128)}, u32[]{:S(2)}) copy-start(s32[1,2,16]{2,1,0:T(2,128)} %param.10) | copy-start | bytes 388
  28.6 2.4 %copy-start = (bf16[1,2,375,375]{3,1,2,0:T(2,128)(2,1)S(1)}, bf16[1,2,375,375]{3,1,2,0:T(2,128)(2,1)}, u32[]{:S(2)}) copy-start(bf16[1,2,375,375]{3,1,2,0:T(2,128)(2,1)} %param.12) | copy-start | bytes 1687504
  29.4 3.0 %collective-permute-start.10 = (bf16[3,375,256]{2,1,0:T(8,128)(2,1)S(1)}, bf16[3,375,256]{2,1,0:T(8,128)(2,1)S(1)}, u32[]{:S(2)}, u32[]{:S(2)}) collective-permute-start(bf16[3,375,256]{2,1,0:T(8,128)(2,1)S(1)} %get-tuple-element.83.mine_ref), channel_id=1, source_target_pairs={{0,1},{1,0},{2,3},{3,2},{4,5},{5,4},{6,7},{7,6},{8,9},{9,8},{10,11... | collective-permute-start | bytes 1728008 | tf_op jit(solution)/shard_map/ppermute | solution.py:24
  29.6 7.1 %collective-permute-start.11 = (bf16[375,256]{1,0:T(8,128)(2,1)S(1)}, bf16[375,256]{1,0:T(8,128)(2,1)S(1)}, u32[]{:S(2)}, u32[]{:S(2)}) collective-permute-start(bf16[375,256]{1,0:T(8,128)(2,1)S(1)} %get-tuple-element.79.near_ref), channel_id=1, source_target_pairs={{0,2},{1,3},{2,0},{3,1},{4,5},{5,4},{6,7},{7,6},{8,9},{9,8},{10,11... | collective-permute-start | bytes 576008 | tf_op jit(solution)/shard_map/ppermute | solution.py:24
  30.9 5.8 %collective-permute-start.13 = (bf16[375,256]{1,0:T(8,128)(2,1)S(1)}, bf16[375,256]{1,0:T(8,128)(2,1)S(1)}, u32[]{:S(2)}, u32[]{:S(2)}) collective-permute-start(bf16[375,256]{1,0:T(8,128)(2,1)S(1)} %get-tuple-element.91), channel_id=1, source_target_pairs={{0,1},{1,0},{2,3},{3,2},{4,8},{5,9},{6,10},{7,11},{8,4},{9,5},{10,... | collective-permute-start | bytes 576008 | tf_op jit(solution)/shard_map/ppermute | solution.py:24
  36.7 1.4 %collective-permute-start.12 = (bf16[1,375,256]{2,1,0:T(8,128)(2,1)S(1)}, bf16[1,375,256]{2,1,0:T(8,128)(2,1)S(1)}, u32[]{:S(2)}, u32[]{:S(2)}) collective-permute-start(bf16[1,375,256]{2,1,0:T(8,128)(2,1)S(1)} %bitcast.48), channel_id=1, source_target_pairs={{0,1},{1,0},{2,3},{3,2},{4,5},{5,4},{6,7},{7,6},{8,9},{9,8},{10,11... | collective-permute-start | bytes 576008 | tf_op jit(solution)/shard_map/ppermute | solution.py:24

commit v2 on v1

--- a/solution.py
+++ b/solution.py
@@ -57,13 +57,18 @@
     )
 
 
+def position():
+    here, last = lax.axis_index("sub"), lax.axis_size("sub") - 1
+    return lax.rem(here, 2) == 0, (here == 0) | (here == last), lax.rem(lax.axis_index("blk"), 2) == 1
+
+
 def rows_of(ref, j, part):
     rows, parts, blocks, lanes = ref.shape
     flat = ref.reshape(rows * parts * blocks, lanes)
     return flat, pl.ds(part * blocks + j, rows, stride=parts * blocks)
 
 
-def start_kernel(flags_ref, residual_hbm, *refs):
+def start_kernel(residual_hbm, *refs):
     given = (len(refs) - 5) // 2
     sources, loaded = refs[:given], refs[given : 2 * given]
     scaled_ref, keep_ref, send_ref, residual_ref, sems = refs[2 * given :]
@@ -74,7 +79,7 @@
     ]
     for copy in copies:
         copy.start()
-    is_even, is_edge, is_upper = (flags_ref[i] > 0 for i in range(3))
+    is_even, is_edge, is_upper = position()
     per, _, loads = scaled_ref.shape
     lanes = residual_ref.shape[-1]
     total = jnp.zeros((modes_ref.shape[1], loads), F32)
@@ -180,10 +185,10 @@
     near_bf[...] = near.astype(BF)
 
 
-def far_kernel(flags_ref, fields_ref, near_ref, far_modes, far_in_ref, far_fix_ref, far_out, far_bf, mine_bf):
+def far_kernel(fields_ref, near_ref, far_modes, far_in_ref, far_fix_ref, far_out, far_bf, mine_bf):
     loads = far_fix_ref.shape[-1]
     field = fields_ref[0]
-    scale = jnp.where(flags_ref[1] > 0, 1.0, 0.5).astype(F32)
+    scale = jnp.where(position()[1], 1.0, 0.5).astype(F32)
     far = (far_fix_ref[...] + bdot(far_modes[...], field)) * scale
     far_out[...] = far
     far_bf[...] = far.astype(BF)
@@ -257,9 +262,8 @@
         add_products(list_ref, matrix_ref, sources, values_ref, total_ref)
 
 
-def finish_kernel(list_ref, flags_ref, matrix_ref, picked_ref, total_ref, late_ref, late_core_ref, far_ref, far_in_ref, near_ref, out_ref, sum_ref, values_ref):
-    is_even = flags_ref[0] > 0
-    is_edge = flags_ref[1] > 0
+def finish_kernel(list_ref, matrix_ref, picked_ref, total_ref, late_ref, late_core_ref, far_ref, far_in_ref, near_ref, out_ref, sum_ref, values_ref):
+    is_even, is_edge, _ = position()
 
     @pl.when(is_edge)
     def _():
@@ -324,12 +328,12 @@
         tuple(shape(x.shape, x.dtype) for x in given)
         + (shape((per, block, loads), BF),)
         + (shape((2,) + half_shape, F32),) * 2,
-        [SMEM] + [HBM] * (1 + len(given)),
+        [HBM] * (1 + len(given)),
         2 * per * block * width * loads,
         0,
         [pltpu.VMEM(laid.shape, F32), pltpu.SemaphoreType.DMA((1 + len(given),))],
         52,
-    )(flags, laid, *given)
+    )(laid, *given)
     got = swap(sent, blk=1)
     neumann = turned(neumann_inv)
     near_fix, far_fix, near_modes, far_modes, to_far, mapped_modes = call(
@@ -421,10 +425,10 @@
     far, far_bf, mine_bf = call(
         far_kernel,
         (shape((block, loads), F32), shape((block, loads), BF), shape((count, block, loads), BF)),
-        [SMEM] + [VMEM] * 5,
+        [VMEM] * 5,
         10**11,
         count * block * loads * 8,
-    )(flags, fields, near_bf, far_modes, from_others, far_fix)
+    )(fields, near_bf, far_modes, from_others, far_fix)
 
     core = swap(mine_bf, blk=1)
     picked = call(
@@ -464,14 +468,14 @@
     result = call(
         finish_kernel,
         shape((block, parts, per, lanes), F32),
-        [SMEM, SMEM] + [VMEM] * 8,
+        [SMEM] + [VMEM] * 8,
         2 * block * block * loads,
         block * loads * 16,
         [
             pltpu.VMEM((block, loads), F32),
             pltpu.VMEM((more + 1, block, loads), BF),
         ],
-    )(late_list, flags, matrix, picked, total, late, late_core, far, far_in, near)
+    )(late_list, matrix, picked, total, late, late_core, far, far_in, near)
     return jnp.transpose(result, (2, 0, 1, 3)).reshape(per, block, loads)[None]
 
 

time: 40.9 us -> 40.8 us (level)
  Pallas kernels: 14.4 us -> 13.5 us
  local copies, waits for them, and re-layouts: 5.84 us -> 6.51 us
    unnamed x14 -> x18, local copies, waits for them, and re-layouts: 2.05 us -> 2.72 us
    pallas_call x1, Pallas kernels: 0.8 us -> 0.26 us  [shards(): call(far_kernel, (shape((block, loads), F32), shape((block, loads), BF),...]
    pallas_call x1, Pallas kernels: 2.39 us -> 1.85 us  [shards(): call(start_kernel, tuple((shape(x.shape, x.dtype) for x in given)) + (sha...]
    pallas_call x1, Pallas kernels: 2.57 us -> 3.07 us  [shards(): call(finish_kernel, shape((block, parts, per, lanes), F32), [SMEM] + [VME...]
  transfers between devices with their start and end apart: 14 -> 14, of which waited for: 7 -> 6; matrix products, arithmetic and copies ran while one was open for 9% -> 10% of each run, Pallas kernels for 19% -> 18%
where the time goes in v2:
time: 40.8 us; the launch traced here: 40.7 us
  Pallas kernels  13.5 us (33%)
  starting transfers between devices  13.3 us (33%)
  waiting for transfers between devices  6.89 us (17%)
  local copies, waits for them, and re-layouts  6.51 us (16%)
    ppermute x14, starting transfers between devices, route(): return lax.ppermute(x, ('sub', 'blk'), pairs)  13.3 us
    ppermute x14, waiting for transfers between devices, route(): return lax.ppermute(x, ('sub', 'blk'), pairs)  6.89 us
    dynamic_slice x2, local copies, waits for them, and re-layouts, shards(): lax.dynamic_index_in_dim(stiffness[0], after(far_id, own_bf), 0, False)  3.79 us
    pallas_call x1, Pallas kernels, shards(): call(finish_kernel, shape((block, parts, per, lanes), F32), [SMEM] + [VME...  3.07 us
    unnamed x18, local copies, waits for them, and re-layouts  2.72 us
    pallas_call x1, Pallas kernels, shards(): call(functools.partial(couple_kernel, more), (shape((block, loads), F32),...  2.5 us
    pallas_call x1, Pallas kernels, shards(): call(start_kernel, tuple((shape(x.shape, x.dtype) for x in given)) + (sha...  1.85 us
    pallas_call x1, Pallas kernels, shards(): call(local_kernel, (shape((block, loads), F32),) * 2 + (shape((block, wid...  1.73 us
  transfers between devices with their start and end apart: 14, of which 6 were waited for; matrix products, arithmetic and copies ran while one was open for 10% of the time, Pallas kernels for 18%

profile of v2, /device:TPU:0, one launch (start us, length us, event | category | flops | bytes accessed | tf_op | source)
XLA Modules:
  0.0 40.7 jit_solution(6156908134523648953)
XLA Ops:
  0.0 1.0 %copy-done.1 = bf16[1,2,375,192]{2,3,1,0:T(8,128)(2,1)S(1)} copy-done((bf16[1,2,375,192]{2,3,1,0:T(8,128)(2,1)S(1)}, bf16[1,2,375,192]{2,3,1,0:T(8,128)(2,1)}, u32[]{:S(2)}) %copy-start.1) | copy-done | bytes 288024
  1.0 1.8 %shard_map.82 = (bf16[2,192,375]{2,1,0:T(8,128)(2,1)S(1)}, f32[3,192,192]{2,1,0:T(8,128)S(1)}, bf16[2,375,256]{2,1,0:T(8,128)(2,1)S(1)}, f32[2,192,128]{2,1,0:T(8,128)S(1)}, f32[2,192,128]{2,1,0:T(8,128)S(1)}) custom-call(f32[375,2,2,128]{3,2,1,0:T(2,128)} %bitcast.53, bf16[2,192,375]{2,1,0:T(8,128)(2,1)S(1)} %bitcast.47, f32[3,192,192]{2,1,0:T(8,128)} %bitcast.54), custom_call_target="tpu_custom_call" | custom-call | flops 73728000 | tf_op jit(solution)/shard_map/pallas_call | solution.py:326
  2.8 0.5 %collective-permute-start = (f32[2,192,128]{2,1,0:T(8,128)S(1)}, f32[2,192,128]{2,1,0:T(8,128)S(1)}, u32[]{:S(2)}, u32[]{:S(2)}) collective-permute-start(f32[2,192,128]{2,1,0:T(8,128)S(1)} %get-tuple-element.50), channel_id=1, source_target_pairs={{0,1},{1,0},{2,3},{3,2},{4,5},{5,4},{6,7},{7,6},{8,9},{9,8},{10,11... | collective-permute-start | bytes 589832 | tf_op jit(solution)/shard_map/ppermute | solution.py:24
  3.4 1.0 %collective-permute-done.got_ref = f32[2,192,128]{2,1,0:T(8,128)S(1)} collective-permute-done((f32[2,192,128]{2,1,0:T(8,128)S(1)}, f32[2,192,128]{2,1,0:T(8,128)S(1)}, u32[]{:S(2)}, u32[]{:S(2)}) %collective-permute-start) | collective-permute-done | bytes 196640 | tf_op jit(solution)/shard_map/ppermute | solution.py:24
  4.4 3.9 %collective-permute-start.3 = (bf16[192,128]{1,0:T(8,128)(2,1)S(1)}, bf16[192,128]{1,0:T(8,128)(2,1)S(1)}, u32[]{:S(2)}, u32[]{:S(2)}) collective-permute-start(bf16[192,128]{1,0:T(8,128)(2,1)S(1)} %get-tuple-element.93), channel_id=1, source_target_pairs={{0,6},{1,7},{2,4},{3,5},{4,2},{5,3},{6,0},{7,1},{8,14},{9,15},{10,... | collective-permute-start | bytes 147464 | tf_op jit(solution)/shard_map/ppermute | solution.py:24
  8.3 0.5 %collective-permute-start.2 = (bf16[192,128]{1,0:T(8,128)(2,1)S(1)}, bf16[192,128]{1,0:T(8,128)(2,1)S(1)}, u32[]{:S(2)}, u32[]{:S(2)}) collective-permute-start(bf16[192,128]{1,0:T(8,128)(2,1)S(1)} %get-tuple-element.93), channel_id=1, source_target_pairs={{0,4},{1,5},{2,6},{3,7},{4,0},{5,1},{6,2},{7,3},{8,12},{9,13},{10,... | collective-permute-start | bytes 147464 | tf_op jit(solution)/shard_map/ppermute | solution.py:24
  9.0 1.1 %copy-done.3 = bf16[1,2,375,375]{3,1,2,0:T(2,128)(2,1)S(1)} copy-done((bf16[1,2,375,375]{3,1,2,0:T(2,128)(2,1)S(1)}, bf16[1,2,375,375]{3,1,2,0:T(2,128)(2,1)}, u32[]{:S(2)}) %copy-start.3) | copy-done | bytes 562524
  10.0 1.7 %shard_map.83 = (f32[375,256]{1,0:T(8,128)S(1)}, f32[375,256]{1,0:T(8,128)S(1)}, bf16[375,192]{1,0:T(8,128)(2,1)S(1)}, bf16[375,192]{1,0:T(8,128)(2,1)S(1)}, bf1...) custom-call(s32[3]{0:T(128)S(1)} %add_convert_fusion.flags_ref, ...), custom_call_target="tpu_custom_call" | custom-call | flops 99999997952 | tf_op jit(solution)/shard_map/pallas_call | solution.py:339
  11.8 0.7 %copy-done.6 = bf16[375,192]{1,0:T(8,128)(2,1)} copy-done((bf16[375,192]{1,0:T(8,128)(2,1)}, bf16[375,192]{1,0:T(8,128)(2,1)S(1)}, u32[]{:S(2)}) %copy-start.6) | copy-done | bytes 144024
  12.9 0.6 %shard_map.84 = (f32[192,128]{1,0:T(8,128)S(1)}, f32[192,128]{1,0:T(8,128)S(1)}, f32[192,128]{1,0:T(8,128)S(1)}, bf16[192,128]{1,0:T(8,128)(2,1)S(1)}, bf16[192,128]{1,0:T(8,128)(2,1)S(1)}) custom-call(f32[2,192,128]{2,1,0:T(8,128)S(1)} %get-tuple-element.49.keep_ref, f32[2,192,128]{2,1,0:T(8,128)S(1)} %collective-permute-done.got_ref, ...), custom_call_target="tpu_custom_call" | custom-call | flops 28311552 | bytes 294912 | tf_op jit(solution)/shard_map/pallas_call | solution.py:359
  13.6 1.6 %collective-permute-start.4 = (bf16[192,128]{1,0:T(8,128)(2,1)S(1)}, bf16[192,128]{1,0:T(8,128)(2,1)S(1)}, u32[]{:S(2)}, u32[]{:S(2)}) collective-permute-start(bf16[192,128]{1,0:T(8,128)(2,1)S(1)} %get-tuple-element.59), channel_id=1, source_target_pairs={{0,8},{1,9},{2,10},{3,11},{4,12},{5,13},{6,14},{7,15},{8,0},{9,1},... | collective-permute-start | bytes 147464 | tf_op jit(solution)/shard_map/ppermute | solution.py:24
  15.3 1.4 %collective-permute-start.8 = (bf16[448,375]{1,0:T(8,128)(2,1)S(1)}, bf16[448,375]{1,0:T(8,128)(2,1)S(1)}, u32[]{:S(2)}, u32[]{:S(2)}) collective-permute-start(bf16[448,375]{1,0:T(8,128)(2,1)S(1)} %get-tuple-element.69), channel_id=1, source_target_pairs={{0,2},{1,3},{2,0},{3,1},{4,6},{5,7},{6,4},{7,5},{8,10},{9,11},{10,... | collective-permute-start | bytes 1008008 | tf_op jit(solution)/shard_map/ppermute | solution.py:24
  17.1 1.6 %collective-permute-start.7 = (bf16[448,375]{1,0:T(8,128)(2,1)S(1)}, bf16[448,375]{1,0:T(8,128)(2,1)S(1)}, u32[]{:S(2)}, u32[]{:S(2)}) collective-permute-start(bf16[448,375]{1,0:T(8,128)(2,1)S(1)} %shard_map.87), channel_id=1, source_target_pairs={{0,4},{1,5},{2,6},{3,7},{4,0},{5,1},{6,2},{7,3},{8,12},{9,13},{10,... | collective-permute-start | bytes 1008008 | tf_op jit(solution)/shard_map/ppermute | solution.py:24
  18.9 2.6 %collective-permute-start.5 = (bf16[192,128]{1,0:T(8,128)(2,1)S(1)}, bf16[192,128]{1,0:T(8,128)(2,1)S(1)}, u32[]{:S(2)}, u32[]{:S(2)}) collective-permute-start(bf16[192,128]{1,0:T(8,128)(2,1)S(1)} %get-tuple-element.61), channel_id=1, source_target_pairs={{0,16},{1,17},{2,18},{3,19},{4,20},{5,21},{6,22},{7,23},{8,24},{9,... | collective-permute-start | bytes 147464 | tf_op jit(solution)/shard_map/ppermute | solution.py:24
  21.6 2.8 %constant_dynamic-slice_fusion = bf16[1,1,16,375,375]{4,2,3,1,0:T(8,128)(2,1)S(1)} fusion(bf16[1,2,16,375,375]{4,2,3,1,0:T(8,128)(2,1)} %param.9, s32[]{:T(128)S(6)} %select_n.88), kind=kLoop, calls=%fused_computation.30 | loop fusion | bytes 9000004 | tf_op jit(solution)/shard_map/jit(dynamic_index_in_dim)/dynamic_slice | solution.py:397
  24.3 1.0 %copy.11 = bf16[1,1,16,375,375]{4,3,2,1,0:T(8,128)(2,1)S(1)} copy(bf16[1,1,16,375,375]{4,2,3,1,0:T(8,128)(2,1)S(1)} %constant_dynamic-slice_fusion) | data formatting | bytes 9000000 | tf_op jit(solution)/shard_map/jit(dynamic_index_in_dim)/dynamic_slice | solution.py:397
  25.4 1.0 %shard_map.86 = bf16[2,192,128]{2,1,0:T(8,128)(2,1)S(1)} custom-call(f32[192,128]{1,0:T(8,128)S(1)} %get-tuple-element.60.own_ref, bf16[192,128]{1,0:T(8,128)(2,1)S(1)} %collective-permute-done.5.got_ref, f32[3,192,192]{2,1,0:T(8,128)S(1)} %get-tuple-element.54.map_ref, f32[192,192]{1,0:T(8,128)S(1)} %copy-done.2, ...), custom_call_target="tpu_custom_call" | custom-call | flops 56623104 | bytes 737280 | tf_op jit(solution)/shard_map/pallas_call | solution.py:388
  27.2 1.0 %collective-permute-done.9 = bf16[2,192,128]{2,1,0:T(8,128)(2,1)S(1)} collective-permute-done((bf16[2,192,128]{2,1,0:T(8,128)(2,1)S(1)}, bf16[2,192,128]{2,1,0:T(8,128)(2,1)S(1)}, u32[]{:S(2)}, u32[]{:S(2)}) %collective-permute-start.9) | collective-permute-done | bytes 98336 | tf_op jit(solution)/shard_map/ppermute | solution.py:24
  29.1 0.6 %collective-permute-start.11 = (bf16[375,256]{1,0:T(8,128)(2,1)S(1)}, bf16[375,256]{1,0:T(8,128)(2,1)S(1)}, u32[]{:S(2)}, u32[]{:S(2)}) collective-permute-start(bf16[375,256]{1,0:T(8,128)(2,1)S(1)} %get-tuple-element.79.near_ref), channel_id=1, source_target_pairs={{0,2},{1,3},{2,0},{3,1},{4,5},{5,4},{6,7},{7,6},{8,9},{9,8},{10,11... | collective-permute-start | bytes 576008 | tf_op jit(solution)/shard_map/ppermute | solution.py:24
  29.9 1.4 %shard_map.92.picked_ref = bf16[375,375]{1,0:T(8,128)(2,1)S(1)} custom-call(s32[3]{0:T(128)S(1)} %add_convert_fusion.flags_ref, bf16[375,2,375]{2,1,0:T(2,128)(2,1)S(1)} %bitcast.46), custom_call_target="tpu_custom_call" | custom-call | flops 1000 | tf_op jit(solution)/shard_map/pallas_call | solution.py:434
  31.2 2.5 %shard_map.91 = (f32[375,256]{1,0:T(8,128)S(1)}, s32[3,16]{1,0:T(4,128)S(1)}) custom-call(s32[16]{0:T(128)S(1)} %and_select_fusion.1.slots_ref, s32[3]{0:T(128)S(1)} %add_convert_fusion.flags_ref, bf16[16,375,375]{2,1,0:T(8,128)(2,1)S(1)} %bitcast.44, bf16[3,375,256]{2,1,0:T(8,128)(2,1)S(1)} %get-tuple-element.83.mine_ref, ...), custom_call_target="tpu_custom_call" | custom-call | flops 1000 | bytes 4500000 | tf_op jit(solution)/shard_map/pallas_call | solution.py:457
  33.8 2.4 %collective-permute-done.11 = bf16[375,256]{1,0:T(8,128)(2,1)S(1)} collective-permute-done((bf16[375,256]{1,0:T(8,128)(2,1)S(1)}, bf16[375,256]{1,0:T(8,128)(2,1)S(1)}, u32[]{:S(2)}, u32[]{:S(2)}) %collective-permute-start.11) | collective-permute-done | bytes 192032 | tf_op jit(solution)/shard_map/ppermute | solution.py:24
  36.2 1.4 %collective-permute-done.12.late_core_ref = bf16[1,375,256]{2,1,0:T(8,128)(2,1)S(1)} collective-permute-done((bf16[1,375,256]{2,1,0:T(8,128)(2,1)S(1)}, bf16[1,375,256]{2,1,0:T(8,128)(2,1)S(1)}, u32[]{:S(2)}, u32[]{:S(2)}) %collective-permute-start.12) | collective-permute-done | bytes 192032 | tf_op jit(solution)/shard_map/ppermute | solution.py:24
  37.6 3.1 %shard_map.93 = f32[375,2,2,128]{3,2,1,0:T(2,128)} custom-call(s32[3,16]{1,0:T(4,128)S(1)} %get-tuple-element.84.list_ref, bf16[16,375,375]{2,1,0:T(8,128)(2,1)S(1)} %bitcast.45, bf16[375,375]{1,0:T(8,128)(2,1)S(1)} %shard_map.92.picked_ref, f32[375,256]{1,0:T(8,128)S(1)} %get-tuple-element.88.total_ref, bf16[1,375,256]{2,1,0:T(8,128)(2,1)S(1)} %bitcast.49, ...), custom_call_target="tpu_custom_call" | custom-call | flops 72000000 | bytes 1536000 | tf_op jit(solution)/shard_map/pallas_call | solution.py:468
  (44 shorter events, 3.1 us)
Async XLA Ops:
  0.0 1.0 %copy-start.1 = (bf16[1,2,375,192]{2,3,1,0:T(8,128)(2,1)S(1)}, bf16[1,2,375,192]{2,3,1,0:T(8,128)(2,1)}, u32[]{:S(2)}) copy-start(bf16[1,2,375,192]{2,3,1,0:T(8,128)(2,1)} %param.13) | copy-start | bytes 864004
  2.8 1.6 %collective-permute-start = (f32[2,192,128]{2,1,0:T(8,128)S(1)}, f32[2,192,128]{2,1,0:T(8,128)S(1)}, u32[]{:S(2)}, u32[]{:S(2)}) collective-permute-start(f32[2,192,128]{2,1,0:T(8,128)S(1)} %get-tuple-element.50), channel_id=1, source_target_pairs={{0,1},{1,0},{2,3},{3,2},{4,5},{5,4},{6,7},{7,6},{8,9},{9,8},{10,11... | collective-permute-start | bytes 589832 | tf_op jit(solution)/shard_map/ppermute | solution.py:24
  4.4 8.0 %collective-permute-start.3 = (bf16[192,128]{1,0:T(8,128)(2,1)S(1)}, bf16[192,128]{1,0:T(8,128)(2,1)S(1)}, u32[]{:S(2)}, u32[]{:S(2)}) collective-permute-start(bf16[192,128]{1,0:T(8,128)(2,1)S(1)} %get-tuple-element.93), channel_id=1, source_target_pairs={{0,6},{1,7},{2,4},{3,5},{4,2},{5,3},{6,0},{7,1},{8,14},{9,15},{10,... | collective-permute-start | bytes 147464 | tf_op jit(solution)/shard_map/ppermute | solution.py:24
  8.3 4.1 %collective-permute-start.2 = (bf16[192,128]{1,0:T(8,128)(2,1)S(1)}, bf16[192,128]{1,0:T(8,128)(2,1)S(1)}, u32[]{:S(2)}, u32[]{:S(2)}) collective-permute-start(bf16[192,128]{1,0:T(8,128)(2,1)S(1)} %get-tuple-element.93), channel_id=1, source_target_pairs={{0,4},{1,5},{2,6},{3,7},{4,0},{5,1},{6,2},{7,3},{8,12},{9,13},{10,... | collective-permute-start | bytes 147464 | tf_op jit(solution)/shard_map/ppermute | solution.py:24
  8.8 4.1 %collective-permute-start.1 = (bf16[192,128]{1,0:T(8,128)(2,1)S(1)}, bf16[192,128]{1,0:T(8,128)(2,1)S(1)}, u32[]{:S(2)}, u32[]{:S(2)}) collective-permute-start(bf16[192,128]{1,0:T(8,128)(2,1)S(1)} %get-tuple-element.94), channel_id=1, source_target_pairs={{0,2},{1,3},{2,0},{3,1},{4,6},{5,7},{6,4},{7,5},{8,10},{9,11},{10,... | collective-permute-start | bytes 147464 | tf_op jit(solution)/shard_map/ppermute | solution.py:24
  9.0 1.1 %copy-start.3 = (bf16[1,2,375,375]{3,1,2,0:T(2,128)(2,1)S(1)}, bf16[1,2,375,375]{3,1,2,0:T(2,128)(2,1)}, u32[]{:S(2)}) copy-start(bf16[1,2,375,375]{3,1,2,0:T(2,128)(2,1)} %param.11) | copy-start | bytes 1687504
  11.8 0.7 %copy-start.6 = (bf16[375,192]{1,0:T(8,128)(2,1)}, bf16[375,192]{1,0:T(8,128)(2,1)S(1)}, u32[]{:S(2)}) copy-start(bf16[375,192]{1,0:T(8,128)(2,1)S(1)} %get-tuple-element.80.far_modes) | copy-start | bytes 432004
  12.4 4.3 %copy-start.4 = (f32[375,256]{1,0:T(8,128)}, f32[375,256]{1,0:T(8,128)S(1)}, u32[]{:S(2)}) copy-start(f32[375,256]{1,0:T(8,128)S(1)} %get-tuple-element.82.far_fix_ref) | copy-start | bytes 1152004
  13.5 3.2 %collective-permute-start.6 = (bf16[192,128]{1,0:T(8,128)(2,1)S(1)}, bf16[192,128]{1,0:T(8,128)(2,1)S(1)}, u32[]{:S(2)}, u32[]{:S(2)}) collective-permute-start(bf16[192,128]{1,0:T(8,128)(2,1)S(1)} %get-tuple-element.65), channel_id=1, source_target_pairs={{0,1},{1,0},{2,3},{3,2},{4,5},{5,4},{6,7},{7,6},{8,9},{9,8},{10,11... | collective-permute-start | bytes 147464 | tf_op jit(solution)/shard_map/ppermute | solution.py:24
  13.6 5.0 %collective-permute-start.4 = (bf16[192,128]{1,0:T(8,128)(2,1)S(1)}, bf16[192,128]{1,0:T(8,128)(2,1)S(1)}, u32[]{:S(2)}, u32[]{:S(2)}) collective-permute-start(bf16[192,128]{1,0:T(8,128)(2,1)S(1)} %get-tuple-element.59), channel_id=1, source_target_pairs={{0,8},{1,9},{2,10},{3,11},{4,12},{5,13},{6,14},{7,15},{8,0},{9,1},... | collective-permute-start | bytes 147464 | tf_op jit(solution)/shard_map/ppermute | solution.py:24
  15.3 11.2 %collective-permute-start.8 = (bf16[448,375]{1,0:T(8,128)(2,1)S(1)}, bf16[448,375]{1,0:T(8,128)(2,1)S(1)}, u32[]{:S(2)}, u32[]{:S(2)}) collective-permute-start(bf16[448,375]{1,0:T(8,128)(2,1)S(1)} %get-tuple-element.69), channel_id=1, source_target_pairs={{0,2},{1,3},{2,0},{3,1},{4,6},{5,7},{6,4},{7,5},{8,10},{9,11},{10,... | collective-permute-start | bytes 1008008 | tf_op jit(solution)/shard_map/ppermute | solution.py:24
  17.1 9.9 %collective-permute-start.7 = (bf16[448,375]{1,0:T(8,128)(2,1)S(1)}, bf16[448,375]{1,0:T(8,128)(2,1)S(1)}, u32[]{:S(2)}, u32[]{:S(2)}) collective-permute-start(bf16[448,375]{1,0:T(8,128)(2,1)S(1)} %shard_map.87), channel_id=1, source_target_pairs={{0,4},{1,5},{2,6},{3,7},{4,0},{5,1},{6,2},{7,3},{8,12},{9,13},{10,... | collective-permute-start | bytes 1008008 | tf_op jit(solution)/shard_map/ppermute | solution.py:24
  18.9 6.5 %collective-permute-start.5 = (bf16[192,128]{1,0:T(8,128)(2,1)S(1)}, bf16[192,128]{1,0:T(8,128)(2,1)S(1)}, u32[]{:S(2)}, u32[]{:S(2)}) collective-permute-start(bf16[192,128]{1,0:T(8,128)(2,1)S(1)} %get-tuple-element.61), channel_id=1, source_target_pairs={{0,16},{1,17},{2,18},{3,19},{4,20},{5,21},{6,22},{7,23},{8,24},{9,... | collective-permute-start | bytes 147464 | tf_op jit(solution)/shard_map/ppermute | solution.py:24
  24.3 1.1 %copy-start.2 = (f32[192,192]{1,0:T(8,128)S(1)}, f32[192,192]{1,0:T(8,128)}, u32[]{:S(2)}) copy-start(f32[192,192]{1,0:T(8,128)} %root_ref.1) | copy-start | bytes 442372
  25.4 3.2 %copy-start.5 = (f32[375,256]{1,0:T(8,128)S(1)}, f32[375,256]{1,0:T(8,128)}, u32[]{:S(2)}) copy-start(f32[375,256]{1,0:T(8,128)} %copy-done.4) | copy-start | bytes 1152004
  25.4 3.2 %copy-start.7 = (bf16[375,192]{1,0:T(8,128)(2,1)S(1)}, bf16[375,192]{1,0:T(8,128)(2,1)}, u32[]{:S(2)}) copy-start(bf16[375,192]{1,0:T(8,128)(2,1)} %copy-done.6) | copy-start | bytes 432004
  27.0 1.3 %collective-permute-start.9 = (bf16[2,192,128]{2,1,0:T(8,128)(2,1)S(1)}, bf16[2,192,128]{2,1,0:T(8,128)(2,1)S(1)}, u32[]{:S(2)}, u32[]{:S(2)}) collective-permute-start(bf16[2,192,128]{2,1,0:T(8,128)(2,1)S(1)} %shard_map.86), channel_id=1, source_target_pairs={{0,1},{1,0},{2,3},{3,2},{4,5},{5,4},{6,7},{7,6},{8,9},{9,8},{10,11... | collective-permute-start | bytes 294920 | tf_op jit(solution)/shard_map/ppermute | solution.py:24
  28.6 1.1 %copy-start.8 = (s32[1,2,16]{2,1,0:T(2,128)S(1)}, s32[1,2,16]{2,1,0:T(2,128)}, u32[]{:S(2)}) copy-start(s32[1,2,16]{2,1,0:T(2,128)} %param.10) | copy-start | bytes 388
  28.6 1.2 %copy-start = (bf16[1,2,375,375]{3,1,2,0:T(2,128)(2,1)S(1)}, bf16[1,2,375,375]{3,1,2,0:T(2,128)(2,1)}, u32[]{:S(2)}) copy-start(bf16[1,2,375,375]{3,1,2,0:T(2,128)(2,1)} %param.12) | copy-start | bytes 1687504
  28.9 2.3 %collective-permute-start.10 = (bf16[3,375,256]{2,1,0:T(8,128)(2,1)S(1)}, bf16[3,375,256]{2,1,0:T(8,128)(2,1)S(1)}, u32[]{:S(2)}, u32[]{:S(2)}) collective-permute-start(bf16[3,375,256]{2,1,0:T(8,128)(2,1)S(1)} %get-tuple-element.83.mine_ref), channel_id=1, source_target_pairs={{0,1},{1,0},{2,3},{3,2},{4,5},{5,4},{6,7},{7,6},{8,9},{9,8},{10,11... | collective-permute-start | bytes 1728008 | tf_op jit(solution)/shard_map/ppermute | solution.py:24
  29.1 7.1 %collective-permute-start.11 = (bf16[375,256]{1,0:T(8,128)(2,1)S(1)}, bf16[375,256]{1,0:T(8,128)(2,1)S(1)}, u32[]{:S(2)}, u32[]{:S(2)}) collective-permute-start(bf16[375,256]{1,0:T(8,128)(2,1)S(1)} %get-tuple-element.79.near_ref), channel_id=1, source_target_pairs={{0,2},{1,3},{2,0},{3,1},{4,5},{5,4},{6,7},{7,6},{8,9},{9,8},{10,11... | collective-permute-start | bytes 576008 | tf_op jit(solution)/shard_map/ppermute | solution.py:24
  29.7 6.5 %collective-permute-start.13 = (bf16[375,256]{1,0:T(8,128)(2,1)S(1)}, bf16[375,256]{1,0:T(8,128)(2,1)S(1)}, u32[]{:S(2)}, u32[]{:S(2)}) collective-permute-start(bf16[375,256]{1,0:T(8,128)(2,1)S(1)} %get-tuple-element.91), channel_id=1, source_target_pairs={{0,1},{1,0},{2,3},{3,2},{4,8},{5,9},{6,10},{7,11},{8,4},{9,5},{10,... | collective-permute-start | bytes 576008 | tf_op jit(solution)/shard_map/ppermute | solution.py:24
  36.2 1.4 %collective-permute-start.12 = (bf16[1,375,256]{2,1,0:T(8,128)(2,1)S(1)}, bf16[1,375,256]{2,1,0:T(8,128)(2,1)S(1)}, u32[]{:S(2)}, u32[]{:S(2)}) collective-permute-start(bf16[1,375,256]{2,1,0:T(8,128)(2,1)S(1)} %bitcast.48), channel_id=1, source_target_pairs={{0,1},{1,0},{2,3},{3,2},{4,5},{5,4},{6,7},{7,6},{8,9},{9,8},{10,11... | collective-permute-start | bytes 576008 | tf_op jit(solution)/shard_map/ppermute | solution.py:24
